TPU v7x, 256 devices: a whole 4x4x8 slice. The times are simulated.
256 devices in a mesh: video: 2 (over x_lo), frame: 16 (over z, x_hi), head: 8 (over y, core).
Axes of the slice: x: 4 (x_hi: 2, x_lo: 2; x = x_hi * 2 + x_lo), y: 4, z: 8, core: 2. Of those that a mesh axis runs over, the one named last changes fastest.
Arguments:
- query: bfloat16 [49152, 3072], P(('video', 'frame'), 'head'), parts along dimension 0, may hold values from -100 to 100
- keys: bfloat16 [49152, 3072], P(('video', 'frame'), 'head'), parts along dimension 0, may hold values from -4.04 to 4.04
- values: bfloat16 [49152, 3072], P(('video', 'frame'), 'head'), parts along dimension 0, may hold values from -6 to 6
- out_weight: bfloat16 [3072, 3072], P('head'), may hold values from -0.5 to 0.5
- tile_lists: int32 [128, 12], P(('video', 'frame')), parts along dimension 0, may hold values from 0 to 63, as said below
Outputs:
- mixed: bfloat16 [49152, 3072], P(('video', 'frame', 'head')), parts along dimension 0
There are 2 independent parts, one for each index of `video`. A program takes and returns all parts, laid end to end along the dimension named above; an argument that names none is the same for every part. Nothing has to cross between parts.
Inputs may be any that keep to these rules, and one draw needn't show every extreme that they name: `tile_lists`: row t names 12 different tiles; the first is tile t itself, the second lies exactly 2 slabs from tile t's slab, and all lie at most 2 slabs from it (the slab of tile u is u // 4).
All inputs are finite; a program needn't handle non-finite values.
Results may differ from a plain program's by a relative error of at most 0.017.
Values may be sent and summed in bfloat16 or wider, within the bound.
No kernel may reach another device: no remote copies, remote signals or barrier semaphores. Data moves between devices by JAX's collectives and lax.ppermute only.
A program may use at most 192 MiB of HBM per device.

v0:
```python
import math

import jax
import jax.numpy as jnp
from jax import lax
from jax.sharding import PartitionSpec as P

HD = 128
TILE = 384


def shifted(block, axis, distance):
    devices = range(lax.axis_size(axis))
    route = [(i - distance, i) for i in devices if i - distance in devices]
    return lax.ppermute(block, axis, route)


def on_device(query, keys, values, out_weight, tile_lists):
    frames = lax.axis_size("frame")
    my_slab = lax.axis_index("frame")
    reach_slabs = min(2, (frames - 2) // 2)
    col_width = query.shape[1]
    heads_here = col_width // HD
    tokens_here = query.shape[0]
    tiles_here = tokens_here // TILE
    listed = tile_lists.shape[1]
    score_scale = 1.0 / math.sqrt(HD)
    slab_store = {0: (keys, values)}
    for offset in [entry for entry in range(-reach_slabs, reach_slabs + 1) if entry != 0]:
        slab_store[offset] = shifted((keys, values), "frame", -offset)
    ordered = [slab_store[offset] for offset in range(-reach_slabs, reach_slabs + 1)]
    key_bank = jnp.stack([entry_pair[0] for entry_pair in ordered]).reshape(
        -1, TILE, heads_here, HD
    )
    value_bank = jnp.stack([entry_pair[1] for entry_pair in ordered]).reshape(
        -1, TILE, heads_here, HD
    )
    local_ids = (
        tile_lists // tiles_here - my_slab + reach_slabs
    ) * tiles_here + tile_lists % tiles_here
    query_blocks = query.reshape(tiles_here, TILE, heads_here, HD)

    def attend(block):
        query_block, id_row = block
        key_block = key_bank[id_row].reshape(listed * TILE, heads_here, HD)
        value_block = value_bank[id_row].reshape(listed * TILE, heads_here, HD)
        scores = (
            jnp.einsum("qhd,khd->hqk", query_block, key_block, preferred_element_type=jnp.float32)
            * score_scale
        )
        row_max = jnp.max(scores, axis=-1, keepdims=True)
        exp_scores = jnp.exp(scores - row_max)
        row_total = jnp.sum(exp_scores, axis=-1, keepdims=True)
        weights = exp_scores.astype(jnp.bfloat16)
        mixed_block = jnp.einsum(
            "hqk,khd->qhd", weights, value_block, preferred_element_type=jnp.float32
        )
        mixed_block = mixed_block / jnp.transpose(row_total, (1, 0, 2))
        return mixed_block.astype(jnp.bfloat16).reshape(TILE, col_width)

    attended = lax.map(attend, (query_blocks, local_ids)).reshape(tokens_here, col_width)
    return lax.psum_scatter(
        jnp.dot(attended, out_weight, preferred_element_type=jnp.float32).astype(jnp.bfloat16),
        "head",
        scatter_dimension=0,
        tiled=True,
    )


def solution(mesh):
    return jax.shard_map(
        on_device,
        mesh=mesh,
        in_specs=(
            P(("video", "frame"), "head"),
            P(("video", "frame"), "head"),
            P(("video", "frame"), "head"),
            P("head", None),
            P(("video", "frame"), None),
        ),
        out_specs=P(("video", "frame", "head"), None),
        check_vma=False,
    )
```

profile of v0, /device:TPU:1, one launch (start us, length us, event | category | flops | bytes accessed | tf_op | source)
XLA Modules:
  0.0 461.4 jit_solution(10428657856521032512)
XLA Ops:
  6.5 0.0 copy-start
  6.5 5.7 %collective-permute-start = (bf16[1536,384]{1,0:T(8,128)(2,1)}, bf16[1536,384]{1,0:T(8,128)(2,1)}, u32[]{:S(2)}, u32[]{:S(2)}) collective-permute-start(bf16[1536,384]{1,0:T(8,128)(2,1)} %param.9), channel_id=1, source_target_pairs={{0,16},{8,24},{16,32},{24,40},{32,48},{40,56},{48,64},{56,72},{64,... | collective-permute-start | bytes 3538952 | tf_op jit(solution)/shard_map/ppermute | solution.py:15
  12.2 5.7 %collective-permute-start.1 = (bf16[1536,384]{1,0:T(8,128)(2,1)}, bf16[1536,384]{1,0:T(8,128)(2,1)}, u32[]{:S(2)}, u32[]{:S(2)}) collective-permute-start(bf16[1536,384]{1,0:T(8,128)(2,1)} %param.9), channel_id=1, source_target_pairs={{0,8},{8,16},{16,24},{24,32},{32,40},{40,48},{48,56},{56,64},{64,7... | collective-permute-start | bytes 3538952 | tf_op jit(solution)/shard_map/ppermute | solution.py:15
  17.9 1.3 collective-permute-start.2
  19.2 1.3 collective-permute-start.3
  20.5 5.0 %collective-permute-start.4 = (bf16[1536,384]{1,0:T(8,128)(2,1)}, bf16[1536,384]{1,0:T(8,128)(2,1)}, u32[]{:S(2)}, u32[]{:S(2)}) collective-permute-start(bf16[1536,384]{1,0:T(8,128)(2,1)} %param.8), channel_id=1, source_target_pairs={{0,16},{8,24},{16,32},{24,40},{32,48},{40,56},{48,64},{56,72},{64,... | collective-permute-start | bytes 3538952 | tf_op jit(solution)/shard_map/ppermute | solution.py:15
  25.5 4.1 reshape.69
  29.6 2.7 copy.11
  32.3 0.7 fusion.33
  33.0 3.1 collective-permute-done
  36.1 4.7 %collective-permute-start.5 = (bf16[1536,384]{1,0:T(8,128)(2,1)}, bf16[1536,384]{1,0:T(8,128)(2,1)S(1)}, u32[]{:S(2)}, u32[]{:S(2)}) collective-permute-start(bf16[1536,384]{1,0:T(8,128)(2,1)} %param.8), channel_id=1, source_target_pairs={{0,8},{8,16},{16,24},{24,32},{32,40},{40,48},{48,56},{56,64},{64,7... | collective-permute-start | bytes 3538952 | tf_op jit(solution)/shard_map/ppermute | solution.py:15
  40.8 2.4 bitcast_dynamic-update-slice_fusion.9
  43.3 23.5 %collective-permute-done.1 = bf16[1536,384]{1,0:T(8,128)(2,1)} collective-permute-done((bf16[1536,384]{1,0:T(8,128)(2,1)}, bf16[1536,384]{1,0:T(8,128)(2,1)}, u32[]{:S(2)}, u32[]{:S(2)}) %collective-permute-start.1) | collective-permute-done | bytes 1179680 | tf_op jit(solution)/shard_map/ppermute | solution.py:15
  66.8 1.3 collective-permute-start.6
  68.1 2.4 bitcast_dynamic-update-slice_fusion.8
  70.5 1.2 bitcast_dynamic-update-slice_fusion.7
  71.7 0.0 collective-permute-done.4
  71.7 1.3 collective-permute-start.7
  73.0 2.4 bitcast_dynamic-update-slice_fusion.4
  75.4 0.0 collective-permute-done.2
  75.4 2.4 bitcast_dynamic-update-slice_fusion.6
  77.8 0.0 collective-permute-done.3
  77.8 2.4 bitcast_dynamic-update-slice_fusion.5
  80.3 37.1 %collective-permute-done.5 = bf16[1536,384]{1,0:T(8,128)(2,1)S(1)} collective-permute-done((bf16[1536,384]{1,0:T(8,128)(2,1)}, bf16[1536,384]{1,0:T(8,128)(2,1)S(1)}, u32[]{:S(2)}, u32[]{:S(2)}) %collective-permute-start.5) | collective-permute-done | bytes 1179680 | tf_op jit(solution)/shard_map/ppermute | solution.py:15
  117.3 1.1 bitcast_dynamic-update-slice_fusion.3
  118.5 15.8 %reshape.49 = bf16[20,384,3,128]{3,2,1,0:T(4,128)(2,1)} reshape(bf16[5,1536,384]{2,1,0:T(8,128)(2,1)} %bitcast_dynamic-update-slice_fusion.5) | data formatting | bytes 11796480 | tf_op jit(solution)/shard_map/reshape | solution.py:35
  134.3 2.4 bitcast_dynamic-update-slice_fusion.2
  136.7 0.0 collective-permute-done.6
  136.7 2.4 bitcast_dynamic-update-slice_fusion.1
  139.1 0.0 collective-permute-done.7
  139.1 1.2 bitcast_dynamic-update-slice_fusion
  140.3 15.8 %reshape.51 = bf16[20,384,3,128]{3,2,1,0:T(4,128)(2,1)} reshape(bf16[5,1536,384]{2,1,0:T(8,128)(2,1)} %bitcast_dynamic-update-slice_fusion) | data formatting | bytes 11796480 | tf_op jit(solution)/shard_map/reshape | solution.py:32
  156.2 227.0 %while.10 = (s32[]{:T(128)}, bf16[4,384,384]{2,1,0:T(8,128)(2,1)}, s32[4,12]{1,0:T(4,128)S(1)}, bf16[20,384,3,128]{3,2,1,0:T(4,128)(2,1)}, bf16[4,384,3,128]{3,1...) while((s32[]{:T(128)}, bf16[4,384,384]{2,1,0:T(8,128)(2,1)}, s32[4,12]{1,0:T(4,128)S(1)}, ...), condition=%wide.region_3.4_spmd, body=%wide.region_0.3_spmd.sunk | while | flops 2760669952 | bytes 87912256 | solution.py:61
  156.2 10.2 %gather_fusion = bf16[12,384,3,128]{3,2,1,0:T(4,128)(2,1)} fusion(bf16[20,384,3,128]{3,2,1,0:T(4,128)(2,1)} %get-tuple-element.118, s32[1024]{0:T(1024)S(1)} %pad_clamp_fusion.2), kind=kCustom, calls=%fused_computation.1.clone.1 | custom fusion | bytes 7077936 | tf_op jit(solution)/shard_map/while/body/eval_jaxpr/gather | solution.py:45
  166.4 12.4 %multiply_reduce_fusion.2 = (f32[3,384]{1,0:T(4,128)S(1)}, f32[3,384,4608]{2,1,0:T(8,128)}) fusion(bf16[4608,3,128]{2,1,0:T(4,128)(2,1)} %bitcast.66, bf16[4,384,3,128]{3,1,2,0:T(8,128)(2,1)} %get-tuple-element.117, s32[]{:T(128)} %get-tuple-element.106), kind=kOutput, calls=%fused_computation.3.clone.1 | convolution fusion | flops 1369570176 | bytes 26252288 | tf_op jit(solution)/shard_map/while/body/eval_jaxpr/qhd,khd->hqk/dot_general | solution.py:48
  178.8 9.7 %fusion.46 = f32[3,384]{1,0:T(4,128)S(1)} fusion(f32[3,384,4608]{2,1,0:T(8,128)} %get-tuple-element.97, f32[3,384]{1,0:T(4,128)S(1)} %get-tuple-element.98), kind=kLoop, calls=%fused_computation.4.clone.1 | loop fusion | flops 15924096 | bytes 21242880 | tf_op jit(solution)/shard_map/while/body/eval_jaxpr/reduce_sum | solution.py:53
  188.6 10.2 %gather_fusion.1 = bf16[12,384,3,128]{3,2,1,0:T(4,128)(2,1)} fusion(bf16[20,384,3,128]{3,2,1,0:T(4,128)(2,1)} %get-tuple-element.116, s32[1024]{0:T(1024)S(1)} %pad_clamp_fusion.2), kind=kCustom, calls=%fused_computation.clone.1 | custom fusion | bytes 7077936 | tf_op jit(solution)/shard_map/while/body/eval_jaxpr/gather | solution.py:46
  198.8 13.1 %fusion.47 = bf16[384,3,128]{0,2,1:T(8,128)(2,1)S(1)} fusion(f32[3,384,4608]{2,1,0:T(8,128)} %get-tuple-element.97, f32[3,384]{1,0:T(4,128)S(1)} %get-tuple-element.98, bf16[4608,3,128]{2,1,0:T(4,128)(2,1)} %bitcast.67, f32[384,3]{0,1:T(4,128)S(1)} %bitcast.69), kind=kOutput, calls=%fused_computation.14.clone.1 | convolution fusion | flops 1375174656 | bytes 25076736 | tf_op jit(solution)/shard_map/while/body/eval_jaxpr/hqk,khd->qhd/dot_general | solution.py:55
  211.9 0.2 copy.34
  212.2 0.7 constant_dynamic-update-slice_fusion.2
  212.9 10.2 %gather_fusion = bf16[12,384,3,128]{3,2,1,0:T(4,128)(2,1)} fusion(bf16[20,384,3,128]{3,2,1,0:T(4,128)(2,1)} %get-tuple-element.118, s32[1024]{0:T(1024)S(1)} %pad_clamp_fusion.2), kind=kCustom, calls=%fused_computation.1.clone.1 | custom fusion | bytes 7077936 | tf_op jit(solution)/shard_map/while/body/eval_jaxpr/gather | solution.py:45
  223.2 12.4 %multiply_reduce_fusion.2 = (f32[3,384]{1,0:T(4,128)S(1)}, f32[3,384,4608]{2,1,0:T(8,128)}) fusion(bf16[4608,3,128]{2,1,0:T(4,128)(2,1)} %bitcast.66, bf16[4,384,3,128]{3,1,2,0:T(8,128)(2,1)} %get-tuple-element.117, s32[]{:T(128)} %get-tuple-element.106), kind=kOutput, calls=%fused_computation.3.clone.1 | convolution fusion | flops 1369570176 | bytes 26252288 | tf_op jit(solution)/shard_map/while/body/eval_jaxpr/qhd,khd->hqk/dot_general | solution.py:48
  235.6 9.7 %fusion.46 = f32[3,384]{1,0:T(4,128)S(1)} fusion(f32[3,384,4608]{2,1,0:T(8,128)} %get-tuple-element.97, f32[3,384]{1,0:T(4,128)S(1)} %get-tuple-element.98), kind=kLoop, calls=%fused_computation.4.clone.1 | loop fusion | flops 15924096 | bytes 21242880 | tf_op jit(solution)/shard_map/while/body/eval_jaxpr/reduce_sum | solution.py:53
  245.3 10.2 %gather_fusion.1 = bf16[12,384,3,128]{3,2,1,0:T(4,128)(2,1)} fusion(bf16[20,384,3,128]{3,2,1,0:T(4,128)(2,1)} %get-tuple-element.116, s32[1024]{0:T(1024)S(1)} %pad_clamp_fusion.2), kind=kCustom, calls=%fused_computation.clone.1 | custom fusion | bytes 7077936 | tf_op jit(solution)/shard_map/while/body/eval_jaxpr/gather | solution.py:46
  255.6 13.1 %fusion.47 = bf16[384,3,128]{0,2,1:T(8,128)(2,1)S(1)} fusion(f32[3,384,4608]{2,1,0:T(8,128)} %get-tuple-element.97, f32[3,384]{1,0:T(4,128)S(1)} %get-tuple-element.98, bf16[4608,3,128]{2,1,0:T(4,128)(2,1)} %bitcast.67, f32[384,3]{0,1:T(4,128)S(1)} %bitcast.69), kind=kOutput, calls=%fused_computation.14.clone.1 | convolution fusion | flops 1375174656 | bytes 25076736 | tf_op jit(solution)/shard_map/while/body/eval_jaxpr/hqk,khd->qhd/dot_general | solution.py:55
  268.7 0.2 copy.34
  268.9 0.7 constant_dynamic-update-slice_fusion.2
  269.7 10.2 %gather_fusion = bf16[12,384,3,128]{3,2,1,0:T(4,128)(2,1)} fusion(bf16[20,384,3,128]{3,2,1,0:T(4,128)(2,1)} %get-tuple-element.118, s32[1024]{0:T(1024)S(1)} %pad_clamp_fusion.2), kind=kCustom, calls=%fused_computation.1.clone.1 | custom fusion | bytes 7077936 | tf_op jit(solution)/shard_map/while/body/eval_jaxpr/gather | solution.py:45
  279.9 12.4 %multiply_reduce_fusion.2 = (f32[3,384]{1,0:T(4,128)S(1)}, f32[3,384,4608]{2,1,0:T(8,128)}) fusion(bf16[4608,3,128]{2,1,0:T(4,128)(2,1)} %bitcast.66, bf16[4,384,3,128]{3,1,2,0:T(8,128)(2,1)} %get-tuple-element.117, s32[]{:T(128)} %get-tuple-element.106), kind=kOutput, calls=%fused_computation.3.clone.1 | convolution fusion | flops 1369570176 | bytes 26252288 | tf_op jit(solution)/shard_map/while/body/eval_jaxpr/qhd,khd->hqk/dot_general | solution.py:48
  292.4 9.7 %fusion.46 = f32[3,384]{1,0:T(4,128)S(1)} fusion(f32[3,384,4608]{2,1,0:T(8,128)} %get-tuple-element.97, f32[3,384]{1,0:T(4,128)S(1)} %get-tuple-element.98), kind=kLoop, calls=%fused_computation.4.clone.1 | loop fusion | flops 15924096 | bytes 21242880 | tf_op jit(solution)/shard_map/while/body/eval_jaxpr/reduce_sum | solution.py:53
  302.1 10.2 %gather_fusion.1 = bf16[12,384,3,128]{3,2,1,0:T(4,128)(2,1)} fusion(bf16[20,384,3,128]{3,2,1,0:T(4,128)(2,1)} %get-tuple-element.116, s32[1024]{0:T(1024)S(1)} %pad_clamp_fusion.2), kind=kCustom, calls=%fused_computation.clone.1 | custom fusion | bytes 7077936 | tf_op jit(solution)/shard_map/while/body/eval_jaxpr/gather | solution.py:46
  312.3 13.1 %fusion.47 = bf16[384,3,128]{0,2,1:T(8,128)(2,1)S(1)} fusion(f32[3,384,4608]{2,1,0:T(8,128)} %get-tuple-element.97, f32[3,384]{1,0:T(4,128)S(1)} %get-tuple-element.98, bf16[4608,3,128]{2,1,0:T(4,128)(2,1)} %bitcast.67, f32[384,3]{0,1:T(4,128)S(1)} %bitcast.69), kind=kOutput, calls=%fused_computation.14.clone.1 | convolution fusion | flops 1375174656 | bytes 25076736 | tf_op jit(solution)/shard_map/while/body/eval_jaxpr/hqk,khd->qhd/dot_general | solution.py:55
  325.4 0.2 copy.34
  325.7 0.7 constant_dynamic-update-slice_fusion.2
  326.4 10.2 %gather_fusion = bf16[12,384,3,128]{3,2,1,0:T(4,128)(2,1)} fusion(bf16[20,384,3,128]{3,2,1,0:T(4,128)(2,1)} %get-tuple-element.118, s32[1024]{0:T(1024)S(1)} %pad_clamp_fusion.2), kind=kCustom, calls=%fused_computation.1.clone.1 | custom fusion | bytes 7077936 | tf_op jit(solution)/shard_map/while/body/eval_jaxpr/gather | solution.py:45
  336.7 12.4 %multiply_reduce_fusion.2 = (f32[3,384]{1,0:T(4,128)S(1)}, f32[3,384,4608]{2,1,0:T(8,128)}) fusion(bf16[4608,3,128]{2,1,0:T(4,128)(2,1)} %bitcast.66, bf16[4,384,3,128]{3,1,2,0:T(8,128)(2,1)} %get-tuple-element.117, s32[]{:T(128)} %get-tuple-element.106), kind=kOutput, calls=%fused_computation.3.clone.1 | convolution fusion | flops 1369570176 | bytes 26252288 | tf_op jit(solution)/shard_map/while/body/eval_jaxpr/qhd,khd->hqk/dot_general | solution.py:48
  349.1 9.7 %fusion.46 = f32[3,384]{1,0:T(4,128)S(1)} fusion(f32[3,384,4608]{2,1,0:T(8,128)} %get-tuple-element.97, f32[3,384]{1,0:T(4,128)S(1)} %get-tuple-element.98), kind=kLoop, calls=%fused_computation.4.clone.1 | loop fusion | flops 15924096 | bytes 21242880 | tf_op jit(solution)/shard_map/while/body/eval_jaxpr/reduce_sum | solution.py:53
  358.8 10.2 %gather_fusion.1 = bf16[12,384,3,128]{3,2,1,0:T(4,128)(2,1)} fusion(bf16[20,384,3,128]{3,2,1,0:T(4,128)(2,1)} %get-tuple-element.116, s32[1024]{0:T(1024)S(1)} %pad_clamp_fusion.2), kind=kCustom, calls=%fused_computation.clone.1 | custom fusion | bytes 7077936 | tf_op jit(solution)/shard_map/while/body/eval_jaxpr/gather | solution.py:46
  369.1 13.1 %fusion.47 = bf16[384,3,128]{0,2,1:T(8,128)(2,1)S(1)} fusion(f32[3,384,4608]{2,1,0:T(8,128)} %get-tuple-element.97, f32[3,384]{1,0:T(4,128)S(1)} %get-tuple-element.98, bf16[4608,3,128]{2,1,0:T(4,128)(2,1)} %bitcast.67, f32[384,3]{0,1:T(4,128)S(1)} %bitcast.69), kind=kOutput, calls=%fused_computation.14.clone.1 | convolution fusion | flops 1375174656 | bytes 25076736 | tf_op jit(solution)/shard_map/while/body/eval_jaxpr/hqk,khd->qhd/dot_general | solution.py:55
  382.2 0.2 copy.34
  382.4 0.7 constant_dynamic-update-slice_fusion.2
  383.2 8.8 %convolution_convert_fusion = bf16[1536,3072]{1,0:T(8,128)(2,1)} fusion(bf16[1536,384]{1,0:T(8,128)(2,1)} %bitcast.70, bf16[384,3072]{1,0:T(8,128)(2,1)S(1)} %copy-done), kind=kOutput, calls=%fused_computation.25 | convolution fusion | flops 3628597248 | bytes 12976128 | tf_op jit(solution)/shard_map/dot_general | solution.py:63
  391.9 0.0 reduce-scatter.2.cloned.1.call-update
  392.0 62.6 %reduce-scatter.2.cloned.1.call-done = bf16[192,3072]{1,0:T(8,128)(2,1)} async-done(((bf16[1536,3072]{1,0:T(8,128)(2,1)}), bf16[192,3072]{1,0:T(8,128)(2,1)}) %reduce-scatter.2.cloned.1.call-update) | async-done | bytes 1179664 | tf_op jit(solution)/shard_map/reduce_scatter | solution.py:62
  (13 shorter events, 0.1 us)
Async XLA Ops:
  6.5 376.6 %copy-start = (bf16[384,3072]{1,0:T(8,128)(2,1)S(1)}, bf16[384,3072]{1,0:T(8,128)(2,1)}, u32[]{:S(2)}) copy-start(bf16[384,3072]{1,0:T(8,128)(2,1)} %param.10) | copy-start | bytes 7077892
  6.5 64.0 %copy-start.1 = (bf16[1536,384]{1,0:T(8,128)(2,1)S(1)}, bf16[1536,384]{1,0:T(8,128)(2,1)}, u32[]{:S(2)}) copy-start(bf16[1536,384]{1,0:T(8,128)(2,1)} %param.9) | copy-start | bytes 3538948
  6.5 448.1 %reduce-scatter.2.cloned.1.call-start = ((), (), s32[]{:S(2)}) async-start(), calls=%async_computation.1 | async-start | bytes 10616832 | tf_op jit(solution)/shard_map/reduce_scatter | solution.py:62
  6.5 29.6 %collective-permute-start = (bf16[1536,384]{1,0:T(8,128)(2,1)}, bf16[1536,384]{1,0:T(8,128)(2,1)}, u32[]{:S(2)}, u32[]{:S(2)}) collective-permute-start(bf16[1536,384]{1,0:T(8,128)(2,1)} %param.9), channel_id=1, source_target_pairs={{0,16},{8,24},{16,32},{24,40},{32,48},{40,56},{48,64},{56,72},{64,... | collective-permute-start | bytes 3538952 | tf_op jit(solution)/shard_map/ppermute | solution.py:15
  12.2 54.5 %collective-permute-start.1 = (bf16[1536,384]{1,0:T(8,128)(2,1)}, bf16[1536,384]{1,0:T(8,128)(2,1)}, u32[]{:S(2)}, u32[]{:S(2)}) collective-permute-start(bf16[1536,384]{1,0:T(8,128)(2,1)} %param.9), channel_id=1, source_target_pairs={{0,8},{8,16},{16,24},{24,32},{32,40},{40,48},{48,56},{56,64},{64,7... | collective-permute-start | bytes 3538952 | tf_op jit(solution)/shard_map/ppermute | solution.py:15
  17.9 57.5 %collective-permute-start.2 = (bf16[1536,384]{1,0:T(8,128)(2,1)}, bf16[1536,384]{1,0:T(8,128)(2,1)}, u32[]{:S(2)}, u32[]{:S(2)}) collective-permute-start(bf16[1536,384]{1,0:T(8,128)(2,1)} %param.9), channel_id=1, source_target_pairs={{8,0},{16,8},{24,16},{32,24},{40,32},{48,40},{56,48},{64,56},{72,6... | collective-permute-start | bytes 3538952 | tf_op jit(solution)/shard_map/ppermute | solution.py:15
  19.2 58.7 %collective-permute-start.3 = (bf16[1536,384]{1,0:T(8,128)(2,1)}, bf16[1536,384]{1,0:T(8,128)(2,1)}, u32[]{:S(2)}, u32[]{:S(2)}) collective-permute-start(bf16[1536,384]{1,0:T(8,128)(2,1)} %param.9), channel_id=1, source_target_pairs={{16,0},{24,8},{32,16},{40,24},{48,32},{56,40},{64,48},{72,56},{80,... | collective-permute-start | bytes 3538952 | tf_op jit(solution)/shard_map/ppermute | solution.py:15
  20.5 51.2 %collective-permute-start.4 = (bf16[1536,384]{1,0:T(8,128)(2,1)}, bf16[1536,384]{1,0:T(8,128)(2,1)}, u32[]{:S(2)}, u32[]{:S(2)}) collective-permute-start(bf16[1536,384]{1,0:T(8,128)(2,1)} %param.8), channel_id=1, source_target_pairs={{0,16},{8,24},{16,32},{24,40},{32,48},{40,56},{48,64},{56,72},{64,... | collective-permute-start | bytes 3538952 | tf_op jit(solution)/shard_map/ppermute | solution.py:15
  36.1 81.2 %collective-permute-start.5 = (bf16[1536,384]{1,0:T(8,128)(2,1)}, bf16[1536,384]{1,0:T(8,128)(2,1)S(1)}, u32[]{:S(2)}, u32[]{:S(2)}) collective-permute-start(bf16[1536,384]{1,0:T(8,128)(2,1)} %param.8), channel_id=1, source_target_pairs={{0,8},{8,16},{16,24},{24,32},{32,40},{40,48},{48,56},{56,64},{64,7... | collective-permute-start | bytes 3538952 | tf_op jit(solution)/shard_map/ppermute | solution.py:15
  66.8 69.9 %collective-permute-start.6 = (bf16[1536,384]{1,0:T(8,128)(2,1)}, bf16[1536,384]{1,0:T(8,128)(2,1)}, u32[]{:S(2)}, u32[]{:S(2)}) collective-permute-start(bf16[1536,384]{1,0:T(8,128)(2,1)} %param.8), channel_id=1, source_target_pairs={{8,0},{16,8},{24,16},{32,24},{40,32},{48,40},{56,48},{64,56},{72,6... | collective-permute-start | bytes 3538952 | tf_op jit(solution)/shard_map/ppermute | solution.py:15
  71.7 67.4 %collective-permute-start.7 = (bf16[1536,384]{1,0:T(8,128)(2,1)}, bf16[1536,384]{1,0:T(8,128)(2,1)S(1)}, u32[]{:S(2)}, u32[]{:S(2)}) collective-permute-start(bf16[1536,384]{1,0:T(8,128)(2,1)} %param.8), channel_id=1, source_target_pairs={{16,0},{24,8},{32,16},{40,24},{48,32},{56,40},{64,48},{72,56},{80,... | collective-permute-start | bytes 3538952 | tf_op jit(solution)/shard_map/ppermute | solution.py:15
Sparse Core Ops, SparseCore 0:
  392.1 62.4 reduce-scatter.1
where the time goes:
time: 464 us; the launch traced here: 461 us
  local copies, waits for them, and re-layouts  145 us (31%)
  waiting for transfers between devices  126 us (27%)
  matrix products  111 us (24%)
  other arithmetic  39.7 us (9%)
  starting transfers between devices  26.2 us (6%)
  between operations  13.4 us (3%)
    ppermute x8, waiting for transfers between devices, shifted(): return lax.ppermute(block, axis, route)  63.7 us
    reduce_scatter x1, waiting for transfers between devices, on_device(): lax.psum_scatter(jnp.dot(attended, out_weight, preferred_element_type=jnp...  62.6 us
    dot_general x4, matrix products, attend(): jnp.einsum('hqk,khd->qhd', weights, value_block, preferred_element_type=j...  52.5 us
    dot_general x4, matrix products, attend(): jnp.einsum('qhd,khd->hqk', query_block, key_block, preferred_element_type...  49.8 us
    gather x4, local copies, waits for them, and re-layouts, attend(): value_block = value_bank[id_row].reshape(listed * TILE, heads_here, HD)  40.9 us
    gather x4, local copies, waits for them, and re-layouts, attend(): key_block = key_bank[id_row].reshape(listed * TILE, heads_here, HD)  40.9 us
    reduce_sum x4, other arithmetic, attend(): row_total = jnp.sum(exp_scores, axis=-1, keepdims=True)  38.9 us
    ppermute x8, starting transfers between devices, shifted(): return lax.ppermute(block, axis, route)  26.2 us
  transfers between devices with their start and end apart: 9, of which 4 were waited for; matrix products, arithmetic and copies ran while one was open for 9% of the time, Pallas kernels for 0%

commit v1 on v0

v1 whole, which is shorter than its diff:
```python
import functools
import math

import jax
import jax.numpy as jnp
from jax import lax
from jax.experimental import pallas as pl
from jax.experimental.pallas import tpu as pltpu
from jax.sharding import PartitionSpec as P

HD = 128
TILE = 384
CHUNK = 192
SCALE = math.log2(math.e) / math.sqrt(HD)
PLACE = ("frame", "head")


def attend_kernel(ids, q_ref, *refs):
    slabs, (o_ref, key_bank, value_bank, even, odd, sems) = refs[:5], refs[5:]
    tokens = q_ref.shape[0]
    listed = ids.shape[1]
    chunks = tokens // CHUNK
    copies = []
    for i, slab in enumerate(slabs):
        rows = pl.ds(i * tokens, tokens)
        copies.append(
            pltpu.make_async_copy(slab.at[:, 0:HD], key_bank.at[rows, :], sems.at[2 * i])
        )
        copies.append(
            pltpu.make_async_copy(
                slab.at[:, HD : 2 * HD], value_bank.at[rows, 0:HD], sems.at[2 * i + 1]
            )
        )
    for copy in copies:
        copy.start()
    value_bank[:, HD : 2 * HD] = jnp.ones((len(slabs) * tokens, HD), jnp.bfloat16)
    for copy in copies:
        copy.wait()

    def tile_rows(chunk, j):
        return pl.ds(pl.multiple_of(ids[chunk * CHUNK // TILE, j] * TILE, TILE), TILE)

    def chunk_rows(chunk):
        return pl.ds(pl.multiple_of(chunk * CHUNK, CHUNK), CHUNK)

    def score(chunk, store, j):
        tile_scores = lax.dot_general(
            q_ref[chunk_rows(chunk), :],
            key_bank[tile_rows(chunk, j), :],
            (((1,), (1,)), ((), ())),
            preferred_element_type=jnp.float32,
        )
        store[:, j * TILE : (j + 1) * TILE] = tile_scores
        return functools.reduce(
            jnp.maximum, [tile_scores[:, i : i + HD] for i in range(0, TILE, HD)]
        )

    def weigh(chunk, store, j, row_max):
        weights = jnp.exp2(store[:, j * TILE : (j + 1) * TILE] * SCALE - row_max)
        return jnp.dot(
            weights.astype(jnp.bfloat16),
            value_bank[tile_rows(chunk, j), :],
            preferred_element_type=jnp.float32,
        )

    def finish(chunk, total):
        o_ref[chunk_rows(chunk), :] = (total[:, 0:HD] / total[:, HD : 2 * HD]).astype(jnp.bfloat16)

    def row_limit(lane_max):
        return jnp.max(lane_max, axis=1, keepdims=True) * SCALE

    def both(chunk, now, later, row_max):
        lane_max, total = None, None
        for j in range(listed):
            found = score(chunk + 1, later, j)
            lane_max = found if lane_max is None else jnp.maximum(lane_max, found)
            term = weigh(chunk, now, j, row_max)
            total = term if total is None else total + term
        finish(chunk, total)
        return row_limit(lane_max)

    def pair(step, row_max):
        row_max = both(2 * step, even, odd, row_max)
        return both(2 * step + 1, odd, even, row_max)

    row_max = row_limit(
        functools.reduce(jnp.maximum, [score(0, even, j) for j in range(listed)])
    )
    row_max = lax.fori_loop(0, chunks // 2 - 1, pair, row_max)
    row_max = both(chunks - 2, even, odd, row_max)
    total = functools.reduce(
        jnp.add, [weigh(chunks - 1, odd, j, row_max) for j in range(listed)]
    )
    finish(chunks - 1, total)


def attend(ids, query, slabs):
    tokens = query.shape[0]
    listed = ids.shape[1]
    products = tokens * listed * TILE
    in_hbm = pl.BlockSpec(memory_space=pltpu.MemorySpace.HBM)
    in_vmem = pl.BlockSpec(memory_space=pltpu.MemorySpace.VMEM)
    return pl.pallas_call(
        attend_kernel,
        out_shape=jax.ShapeDtypeStruct((tokens, HD), jnp.bfloat16),
        in_specs=[pl.BlockSpec(memory_space=pltpu.MemorySpace.SMEM), in_vmem] + [in_hbm] * 5,
        out_specs=in_vmem,
        scratch_shapes=[
            pltpu.VMEM((5 * tokens, HD), jnp.bfloat16),
            pltpu.VMEM((5 * tokens, 2 * HD), jnp.bfloat16),
            pltpu.VMEM((CHUNK, listed * TILE), jnp.float32),
            pltpu.VMEM((CHUNK, listed * TILE), jnp.float32),
            pltpu.SemaphoreType.DMA((10,)),
        ],
        compiler_params=pltpu.CompilerParams(vmem_limit_bytes=40 * 1024 * 1024),
        cost_estimate=pl.CostEstimate(
            flops=8 * products * HD, bytes_accessed=20 * tokens * HD, transcendentals=products
        ),
    )(ids, query, *slabs)


def on_device(query, keys, values, out_weight, tile_lists):
    frames = lax.axis_size("frame")
    groups = lax.axis_size("head")
    heads_here = query.shape[1] // HD
    tiles_here = query.shape[0] // TILE
    frame = lax.axis_index("frame")
    head = lax.axis_index("head")

    def route(target):
        pairs = []
        for z in range(frames // 2):
            for a in range(2):
                for y in range(groups // 2):
                    for c in range(2):
                        z2, a2, c2 = target(z, a, c)
                        if 0 <= z2 < frames // 2:
                            source = (2 * z + a) * groups + 2 * y + c
                            pairs.append((source, (2 * z2 + a2) * groups + 2 * y + c2))
        return pairs

    turn = route(lambda z, a, c: (z, c, a))
    near = route(lambda z, a, c: (z - 1 if c == 0 else z + 1, a, c))
    far = route(lambda z, a, c: (z + 1 if c == 0 else z - 1, a, c))
    swap = route(lambda z, a, c: (z, a, 1 - c))

    def move(block, pairs):
        return lax.ppermute(block, PLACE, pairs)

    core = head % 2
    slab = frame // 2 * 2 + core
    lists = move(tile_lists, turn)
    offset = lists // tiles_here - slab
    place = jnp.where(
        core == 0,
        jnp.array([4, 3, 0, 1, 2], jnp.int32)[offset + 2],
        jnp.array([2, 1, 0, 3, 4], jnp.int32)[offset + 2],
    )
    ids = place * tiles_here + lists % tiles_here

    columns = [slice(h * HD, (h + 1) * HD) for h in range(heads_here)]
    mixed = None
    for cols in columns:
        own = move(jnp.concatenate([keys[:, cols], values[:, cols]], axis=1), turn)
        turned_query = move(query[:, cols], turn)
        shared = move(own, near)
        other = move(own, swap)
        crossed = move(shared, swap)
        edge = move(own, far)
        attended = attend(ids, turned_query, [own, other, shared, crossed, edge])
        attended = move(attended, turn)
        rows = lax.all_to_all(attended, "head", 0, 1, tiled=True)
        weight = lax.all_gather(out_weight[cols, :], "head", axis=0, tiled=True)
        term = jnp.dot(rows, weight, preferred_element_type=jnp.float32)
        mixed = term if mixed is None else mixed + term
    return mixed.astype(jnp.bfloat16)


def solution(mesh):
    return jax.shard_map(
        on_device,
        mesh=mesh,
        in_specs=(
            P(("video", "frame"), "head"),
            P(("video", "frame"), "head"),
            P(("video", "frame"), "head"),
            P("head", None),
            P(("video", "frame"), None),
        ),
        out_specs=P(("video", "frame", "head"), None),
        check_vma=False,
    )
```

time: 464 us -> 182 us (0.39)
  local copies, waits for them, and re-layouts: 145 us -> 7.99 us
  waiting for transfers between devices: 126 us -> 21.9 us
  matrix products: 111 us -> 17.9 us
  starting transfers between devices: 26.2 us -> 76.4 us
  Pallas kernels: 0 us -> 40.7 us
  other arithmetic: 39.7 us -> 1.62 us
    dot_general x9 -> x3, matrix products: 111 us -> 17.9 us  [on_device(): term = jnp.dot(rows, weight, preferred_element_type=jnp.float32)]
    gather x8 -> x2, local copies, waits for them, and re-layouts: 81.8 us -> 1.55 us  [the longest x1 0.78 us: on_device(): jnp.array([2, 1, 0, 3, 4], jnp.int32)[offset + 2]]
    reduce_scatter x1 -> x0, waiting for transfers between devices: 62.6 us -> none  [on_device(): lax.psum_scatter(jnp.dot(attended, out_weight, preferred_element_type=jnp...]
    ppermute x8 -> x22, waiting for transfers between devices: 63.7 us -> 16.4 us  [move(): return lax.ppermute(block, PLACE, pairs)]
    pallas_call x0 -> x3, Pallas kernels: none -> 40.7 us  [attend(): pl.pallas_call(attend_kernel, out_shape=jax.ShapeDtypeStruct((tokens, HD)...]
    reduce_sum x4 -> x0, other arithmetic: 38.9 us -> none  [attend(): row_total = jnp.sum(exp_scores, axis=-1, keepdims=True)]
    ppermute x8 -> x22, starting transfers between devices: 26.2 us -> 62.8 us  [move(): return lax.ppermute(block, PLACE, pairs)]
    reshape x3 -> x0, local copies, waits for them, and re-layouts: 35.7 us -> none  [the longest x1 15.8 us: on_device(): jnp.stack([entry_pair[0] for entry_pair in ordered])]
  transfers between devices with their start and end apart: 9 -> 28, of which waited for: 4 -> 7; matrix products, arithmetic and copies ran while one was open for 9% -> 10% of each run, Pallas kernels for 0% -> 23%
where the time goes in v1:
time: 182 us; the launch traced here: 180 us
  starting transfers between devices  76.4 us (42%)
  Pallas kernels  40.7 us (22%)
  waiting for transfers between devices  21.9 us (12%)
  matrix products  17.9 us (10%)
  between operations  13.4 us (7%)
  local copies, waits for them, and re-layouts  7.99 us (4%)
    ppermute x22, starting transfers between devices, move(): return lax.ppermute(block, PLACE, pairs)  62.8 us
    pallas_call x3, Pallas kernels, attend(): pl.pallas_call(attend_kernel, out_shape=jax.ShapeDtypeStruct((tokens, HD)...  40.7 us
    dot_general x3, matrix products, on_device(): term = jnp.dot(rows, weight, preferred_element_type=jnp.float32)  17.9 us
    ppermute x22, waiting for transfers between devices, move(): return lax.ppermute(block, PLACE, pairs)  16.4 us
    all_to_all x3, starting transfers between devices, on_device(): rows = lax.all_to_all(attended, 'head', 0, 1, tiled=True)  13.5 us
    all_to_all x3, waiting for transfers between devices, on_device(): rows = lax.all_to_all(attended, 'head', 0, 1, tiled=True)  4.13 us
  transfers between devices with their start and end apart: 28, of which 7 were waited for; matrix products, arithmetic and copies ran while one was open for 10% of the time, Pallas kernels for 23%

profile of v1, /device:TPU:1, one launch (start us, length us, event | category | flops | bytes accessed | tf_op | source)
XLA Modules:
  0.0 180.0 jit_solution(8736105149773015167)
XLA Ops:
  6.5 3.1 %fusion.12 = (bf16[128,3072]{1,0:T(8,128)(2,1)}, bf16[128,3072]{1,0:T(8,128)(2,1)}, bf16[128,3072]{1,0:T(8,128)(2,1)}) fusion(bf16[384,3072]{1,0:T(8,128)(2,1)} %param.10), kind=kLoop, calls=%fused_computation.29 | loop fusion | bytes 4718592 | tf_op jit(solution)/shard_map/slice | solution.py:173
  9.6 0.0 all-gather.4.cloned.1.call-update
  9.7 0.0 all-gather.6.cloned.1.call-start
  9.7 0.7 all-gather.6.cloned.1.call-update
  10.4 0.0 all-gather.8.cloned.1.call-start
  10.4 0.7 all-gather.8.cloned.1.call-update
  11.1 1.5 fusion.13
  12.6 0.0 copy-start.2
  12.7 0.1 pad_maximum_fusion.2
  12.8 6.2 %collective-permute-start.16 = (bf16[1536,256]{1,0:T(8,128)(2,1)S(1)}, bf16[1536,256]{1,0:T(8,128)(2,1)S(1)}, u32[]{:S(2)}, u32[]{:S(2)}) collective-permute-start(bf16[1536,256]{1,0:T(8,128)(2,1)S(1)} %pad_maximum_fusion.2), channel_id=1, source_target_pairs={{0,0},{1,8},{2,2},{3,10},{4,4},{5,12},{6,6},{7,14},{8,1},{9,9},{10... | collective-permute-start | bytes 2359304 | tf_op jit(solution)/shard_map/ppermute | solution.py:148
  18.9 0.1 pad_maximum_fusion
  19.0 0.0 copy-start.6
  19.0 0.0 copy-start.1
  19.1 1.9 %collective-permute-start.2 = (bf16[1536,256]{1,0:T(8,128)(2,1)S(1)}, bf16[1536,256]{1,0:T(8,128)(2,1)S(1)}, u32[]{:S(2)}, u32[]{:S(2)}) collective-permute-start(bf16[1536,256]{1,0:T(8,128)(2,1)S(1)} %pad_maximum_fusion), channel_id=1, source_target_pairs={{0,0},{1,8},{2,2},{3,10},{4,4},{5,12},{6,6},{7,14},{8,1},{9,9},{10... | collective-permute-start | bytes 2359304 | tf_op jit(solution)/shard_map/ppermute | solution.py:148
  21.0 0.1 pad_maximum_fusion.1
  21.1 0.0 copy-start
  21.1 5.1 %collective-permute-start.9 = (bf16[1536,256]{1,0:T(8,128)(2,1)S(1)}, bf16[1536,256]{1,0:T(8,128)(2,1)S(1)}, u32[]{:S(2)}, u32[]{:S(2)}) collective-permute-start(bf16[1536,256]{1,0:T(8,128)(2,1)S(1)} %pad_maximum_fusion.1), channel_id=1, source_target_pairs={{0,0},{1,8},{2,2},{3,10},{4,4},{5,12},{6,6},{7,14},{8,1},{9,9},{10... | collective-permute-start | bytes 2359304 | tf_op jit(solution)/shard_map/ppermute | solution.py:148
  26.2 2.3 %collective-permute-done.16.refs_0_ = bf16[1536,256]{1,0:T(8,128)(2,1)S(1)} collective-permute-done((bf16[1536,256]{1,0:T(8,128)(2,1)S(1)}, bf16[1536,256]{1,0:T(8,128)(2,1)S(1)}, u32[]{:S(2)}, u32[]{:S(2)}) %collective-permute-start.16) | collective-permute-done | bytes 786464 | tf_op jit(solution)/shard_map/ppermute | solution.py:148
  28.6 3.6 %collective-permute-start.18 = (bf16[1536,256]{1,0:T(8,128)(2,1)S(1)}, bf16[1536,256]{1,0:T(8,128)(2,1)S(1)}, u32[]{:S(2)}, u32[]{:S(2)}) collective-permute-start(bf16[1536,256]{1,0:T(8,128)(2,1)S(1)} %collective-permute-done.16.refs_0_), channel_id=1, source_target_pairs={{1,17},{3,19},{5,21},{7,23},{9,25},{11,27},{13,29},{15,31},{16,0},... | collective-permute-start | bytes 2359304 | tf_op jit(solution)/shard_map/ppermute | solution.py:148
  32.2 4.9 %collective-permute-done.2.refs_0_ = bf16[1536,256]{1,0:T(8,128)(2,1)S(1)} collective-permute-done((bf16[1536,256]{1,0:T(8,128)(2,1)S(1)}, bf16[1536,256]{1,0:T(8,128)(2,1)S(1)}, u32[]{:S(2)}, u32[]{:S(2)}) %collective-permute-start.2) | collective-permute-done | bytes 786464 | tf_op jit(solution)/shard_map/ppermute | solution.py:148
  37.1 4.4 %collective-permute-start.4 = (bf16[1536,256]{1,0:T(8,128)(2,1)S(1)}, bf16[1536,256]{1,0:T(8,128)(2,1)}, u32[]{:S(2)}, u32[]{:S(2)}) collective-permute-start(bf16[1536,256]{1,0:T(8,128)(2,1)S(1)} %collective-permute-done.2.refs_0_), channel_id=1, source_target_pairs={{1,17},{3,19},{5,21},{7,23},{9,25},{11,27},{13,29},{15,31},{16,0},... | collective-permute-start | bytes 2359304 | tf_op jit(solution)/shard_map/ppermute | solution.py:148
  41.5 1.1 fusion.15
  42.6 2.0 %collective-permute-start.8 = (bf16[1536,128]{1,0:T(8,128)(2,1)S(1)}, bf16[1536,128]{1,0:T(8,128)(2,1)S(1)}, u32[]{:S(2)}, u32[]{:S(2)}) collective-permute-start(bf16[1536,128]{1,0:T(8,128)(2,1)S(1)} %get-tuple-element.16), channel_id=1, source_target_pairs={{0,0},{1,8},{2,2},{3,10},{4,4},{5,12},{6,6},{7,14},{8,1},{9,9},{10... | collective-permute-start | bytes 1179656 | tf_op jit(solution)/shard_map/ppermute | solution.py:148
  44.6 5.1 %collective-permute-start = (s32[4,12]{1,0:T(4,128)S(1)}, s32[4,12]{1,0:T(4,128)S(1)}, u32[]{:S(2)}, u32[]{:S(2)}) collective-permute-start(s32[4,12]{1,0:T(4,128)S(1)} %copy-done.6), channel_id=1, source_target_pairs={{0,0},{1,8},{2,2},{3,10},{4,4},{5,12},{6,6},{7,14},{8,1},{9,9},{10... | collective-permute-start | bytes 584 | tf_op jit(solution)/shard_map/ppermute | solution.py:148
  49.7 3.6 %collective-permute-done = s32[4,12]{1,0:T(4,128)S(1)} collective-permute-done((s32[4,12]{1,0:T(4,128)S(1)}, s32[4,12]{1,0:T(4,128)S(1)}, u32[]{:S(2)}, u32[]{:S(2)}) %collective-permute-start) | collective-permute-done | bytes 224 | tf_op jit(solution)/shard_map/ppermute | solution.py:148
  53.2 2.8 %collective-permute-start.1 = (bf16[1536,128]{1,0:T(8,128)(2,1)}, bf16[1536,128]{1,0:T(8,128)(2,1)}, u32[]{:S(2)}, u32[]{:S(2)}) collective-permute-start(bf16[1536,128]{1,0:T(8,128)(2,1)} %get-tuple-element.15), channel_id=1, source_target_pairs={{0,0},{1,8},{2,2},{3,10},{4,4},{5,12},{6,6},{7,14},{8,1},{9,9},{10... | collective-permute-start | bytes 1179656 | tf_op jit(solution)/shard_map/ppermute | solution.py:148
  56.1 0.0 collective-permute-done.9.refs_0_
  56.1 4.3 %collective-permute-start.11 = (bf16[1536,256]{1,0:T(8,128)(2,1)S(1)}, bf16[1536,256]{1,0:T(8,128)(2,1)}, u32[]{:S(2)}, u32[]{:S(2)}) collective-permute-start(bf16[1536,256]{1,0:T(8,128)(2,1)S(1)} %collective-permute-done.9.refs_0_), channel_id=1, source_target_pairs={{1,17},{3,19},{5,21},{7,23},{9,25},{11,27},{13,29},{15,31},{16,0},... | collective-permute-start | bytes 2359304 | tf_op jit(solution)/shard_map/ppermute | solution.py:148
  60.4 0.0 collective-permute-done.8.q_ref
  60.4 0.0 collective-permute-start.10
  60.4 3.8 %collective-permute-done.1.q_ref = bf16[1536,128]{1,0:T(8,128)(2,1)} collective-permute-done((bf16[1536,128]{1,0:T(8,128)(2,1)}, bf16[1536,128]{1,0:T(8,128)(2,1)}, u32[]{:S(2)}, u32[]{:S(2)}) %collective-permute-start.1) | collective-permute-done | bytes 393248 | tf_op jit(solution)/shard_map/ppermute | solution.py:148
  64.1 0.0 collective-permute-start.3
  64.1 0.0 collective-permute-done.18.refs_2_
  64.1 1.3 collective-permute-start.6
  65.4 0.0 collective-permute-done.4.refs_2_
  65.4 3.1 %collective-permute-start.5 = (bf16[1536,256]{1,0:T(8,128)(2,1)}, bf16[1536,256]{1,0:T(8,128)(2,1)}, u32[]{:S(2)}, u32[]{:S(2)}) collective-permute-start(bf16[1536,256]{1,0:T(8,128)(2,1)} %collective-permute-done.4.refs_2_), channel_id=1, source_target_pairs={{0,1},{1,0},{2,3},{3,2},{4,5},{5,4},{6,7},{7,6},{8,9},{9,8},{10,11... | collective-permute-start | bytes 2359304 | tf_op jit(solution)/shard_map/ppermute | solution.py:148
  68.5 0.6 reshape.11
  69.2 0.7 pad_clamp_fusion
  69.8 0.8 gather_fusion
  70.6 0.8 gather_fusion.1
  71.4 0.1 reshape.32
  71.5 0.0 collective-permute-done.11.refs_2_
  71.5 1.3 collective-permute-start.13
  72.8 1.9 %collective-permute-start.12 = (bf16[1536,256]{1,0:T(8,128)(2,1)}, bf16[1536,256]{1,0:T(8,128)(2,1)S(1)}, u32[]{:S(2)}, u32[]{:S(2)}) collective-permute-start(bf16[1536,256]{1,0:T(8,128)(2,1)} %collective-permute-done.11.refs_2_), channel_id=1, source_target_pairs={{0,1},{1,0},{2,3},{3,2},{4,5},{5,4},{6,7},{7,6},{8,9},{9,8},{10,11... | collective-permute-start | bytes 2359304 | tf_op jit(solution)/shard_map/ppermute | solution.py:148
  74.7 0.7 fusion.9.ids
  75.4 0.1 collective-permute-start.17
  75.5 1.8 collective-permute-done.6.refs_4_
  77.3 1.3 collective-permute-start.20
  78.6 4.0 %collective-permute-start.19 = (bf16[1536,256]{1,0:T(8,128)(2,1)S(1)}, bf16[1536,256]{1,0:T(8,128)(2,1)}, u32[]{:S(2)}, u32[]{:S(2)}) collective-permute-start(bf16[1536,256]{1,0:T(8,128)(2,1)S(1)} %collective-permute-done.18.refs_2_), channel_id=1, source_target_pairs={{0,1},{1,0},{2,3},{3,2},{4,5},{5,4},{6,7},{7,6},{8,9},{9,8},{10,11... | collective-permute-start | bytes 2359304 | tf_op jit(solution)/shard_map/ppermute | solution.py:148
  82.6 14.1 %shard_map.73 = bf16[1536,128]{1,0:T(8,128)(2,1)S(1)} custom-call(s32[4,12]{1,0:T(4,128)S(1)} %fusion.9.ids, bf16[1536,128]{1,0:T(8,128)(2,1)} %collective-permute-done.1.q_ref, bf16[1536,256]{1,0:T(8,128)(2,1)S(1)} %collective-permute-done.2.refs_0_, bf16[1536,256]{1,0:T(8,128)(2,1)} %collective-permute-done.3.refs_1_, ...), custom_call_target="tpu_custom_call" | custom-call | flops 7247757312 | bytes 3932160 | tf_op jit(solution)/shard_map/pallas_call | solution.py:103
  96.7 3.8 %collective-permute-start.15 = (bf16[1536,128]{1,0:T(8,128)(2,1)}, bf16[1536,128]{1,0:T(8,128)(2,1)S(1)}, u32[]{:S(2)}, u32[]{:S(2)}) collective-permute-start(bf16[1536,128]{1,0:T(8,128)(2,1)} %get-tuple-element.14), channel_id=1, source_target_pairs={{0,0},{1,8},{2,2},{3,10},{4,4},{5,12},{6,6},{7,14},{8,1},{9,9},{10... | collective-permute-start | bytes 1179656 | tf_op jit(solution)/shard_map/ppermute | solution.py:148
  100.6 3.5 %collective-permute-start.7 = (bf16[1536,128]{1,0:T(8,128)(2,1)S(1)}, bf16[1536,128]{1,0:T(8,128)(2,1)S(1)}, u32[]{:S(2)}, u32[]{:S(2)}) collective-permute-start(bf16[1536,128]{1,0:T(8,128)(2,1)S(1)} %shard_map.73), channel_id=1, source_target_pairs={{0,0},{1,8},{2,2},{3,10},{4,4},{5,12},{6,6},{7,14},{8,1},{9,9},{10... | collective-permute-start | bytes 1179656 | tf_op jit(solution)/shard_map/ppermute | solution.py:148
  104.0 13.1 %shard_map.74 = bf16[1536,128]{1,0:T(8,128)(2,1)S(1)} custom-call(s32[4,12]{1,0:T(4,128)S(1)} %fusion.9.ids, bf16[1536,128]{1,0:T(8,128)(2,1)S(1)} %collective-permute-done.8.q_ref, bf16[1536,256]{1,0:T(8,128)(2,1)S(1)} %collective-permute-done.9.refs_0_, bf16[1536,256]{1,0:T(8,128)(2,1)} %collective-permute-done.10.refs_1_, ...), custom_call_target="tpu_custom_call" | custom-call | flops 7247757312 | bytes 3932160 | tf_op jit(solution)/shard_map/pallas_call | solution.py:103
  117.2 3.8 %collective-permute-start.14 = (bf16[1536,128]{1,0:T(8,128)(2,1)S(1)}, bf16[1536,128]{1,0:T(8,128)(2,1)}, u32[]{:S(2)}, u32[]{:S(2)}) collective-permute-start(bf16[1536,128]{1,0:T(8,128)(2,1)S(1)} %shard_map.74), channel_id=1, source_target_pairs={{0,0},{1,8},{2,2},{3,10},{4,4},{5,12},{6,6},{7,14},{8,1},{9,9},{10... | collective-permute-start | bytes 1179656 | tf_op jit(solution)/shard_map/ppermute | solution.py:148
  121.0 4.4 %all-to-all-start = ((bf16[8,192,128]{2,1,0:T(8,128)(2,1)}), bf16[8,192,128]{2,1,0:T(8,128)(2,1)S(1)}, u32[]{:S(2)}, u32[]{:S(2)}) async-start(bf16[8,192,128]{2,1,0:T(8,128)(2,1)} %bitcast.30), calls=%async_computation | async-start | bytes 786432 | tf_op jit(solution)/shard_map/all_to_all | solution.py:172
  125.5 13.4 %shard_map.75 = bf16[1536,128]{1,0:T(8,128)(2,1)S(1)} custom-call(s32[4,12]{1,0:T(4,128)S(1)} %fusion.9.ids, bf16[1536,128]{1,0:T(8,128)(2,1)S(1)} %collective-permute-done.15.q_ref, bf16[1536,256]{1,0:T(8,128)(2,1)S(1)} %collective-permute-done.16.refs_0_, bf16[1536,256]{1,0:T(8,128)(2,1)} %collective-permute-done.17.refs_1_, ...), custom_call_target="tpu_custom_call" | custom-call | flops 7247757312 | bytes 3932160 | tf_op jit(solution)/shard_map/pallas_call | solution.py:103
  138.9 3.3 %collective-permute-start.21 = (bf16[1536,128]{1,0:T(8,128)(2,1)S(1)}, bf16[1536,128]{1,0:T(8,128)(2,1)}, u32[]{:S(2)}, u32[]{:S(2)}) collective-permute-start(bf16[1536,128]{1,0:T(8,128)(2,1)S(1)} %shard_map.75), channel_id=1, source_target_pairs={{0,0},{1,8},{2,2},{3,10},{4,4},{5,12},{6,6},{7,14},{8,1},{9,9},{10... | collective-permute-start | bytes 1179656 | tf_op jit(solution)/shard_map/ppermute | solution.py:148
  142.2 4.9 %all-to-all-start.1 = ((bf16[8,192,128]{2,1,0:T(8,128)(2,1)}), bf16[8,192,128]{2,1,0:T(8,128)(2,1)S(1)}, u32[]{:S(2)}, u32[]{:S(2)}) async-start(bf16[8,192,128]{2,1,0:T(8,128)(2,1)} %bitcast.2), calls=%async_computation.1 | async-start | bytes 786432 | tf_op jit(solution)/shard_map/all_to_all | solution.py:172
  147.1 5.7 %fusion.5 = f32[192,3072]{1,0:T(8,128)} fusion(bf16[1024,3072]{1,0:T(8,128)(2,1)} %all-gather.4.cloned.1.call-done, bf16[8,192,128]{2,1,0:T(8,128)(2,1)S(1)} %all-to-all-done), kind=kOutput, calls=%fused_computation.12 | convolution fusion | flops 1207959552 | bytes 9043968 | tf_op jit(solution)/shard_map/dot_general | solution.py:174
  152.8 2.4 %all-to-all-done.1 = bf16[8,192,128]{2,1,0:T(8,128)(2,1)S(1)} async-done(((bf16[8,192,128]{2,1,0:T(8,128)(2,1)}), bf16[8,192,128]{2,1,0:T(8,128)(2,1)S(1)}, u32[]{:S(2)}, u32[]{:S(2)}) %all-to-all-start.1) | async-done | bytes 393248 | tf_op jit(solution)/shard_map/all_to_all | solution.py:172
  155.2 4.2 %all-to-all-start.2 = ((bf16[8,192,128]{2,1,0:T(8,128)(2,1)}), bf16[8,192,128]{2,1,0:T(8,128)(2,1)S(1)}, u32[]{:S(2)}, u32[]{:S(2)}) async-start(bf16[8,192,128]{2,1,0:T(8,128)(2,1)} %bitcast.4), calls=%async_computation.2 | async-start | bytes 786432 | tf_op jit(solution)/shard_map/all_to_all | solution.py:172
  159.4 6.3 %convolution_add_fusion.1 = f32[192,3072]{1,0:T(8,128)} fusion(f32[192,3072]{1,0:T(8,128)} %fusion.5, bf16[1024,3072]{1,0:T(8,128)(2,1)} %all-gather.6.cloned.1.call-done, bf16[8,192,128]{2,1,0:T(8,128)(2,1)S(1)} %all-to-all-done.1), kind=kOutput, calls=%fused_computation.3 | convolution fusion | flops 1208549376 | bytes 11403264 | tf_op jit(solution)/shard_map/dot_general | solution.py:174
  165.8 1.8 all-to-all-done.2
  167.5 5.9 %fusion = bf16[192,3072]{1,0:T(8,128)(2,1)} fusion(f32[192,3072]{1,0:T(8,128)} %convolution_add_fusion.1, bf16[1024,3072]{1,0:T(8,128)(2,1)} %all-gather.8.cloned.1.call-done, bf16[8,192,128]{2,1,0:T(8,128)(2,1)S(1)} %all-to-all-done.2), kind=kOutput, calls=%fused_computation.4 | convolution fusion | flops 1209139200 | bytes 10223616 | tf_op jit(solution)/shard_map/dot_general | solution.py:174
  (29 shorter events, 0.1 us)
Async XLA Ops:
  6.5 140.6 %all-gather.4.cloned.1.call-start = ((), (), s32[]{:S(2)}) async-start(), calls=%async_computation.3 | async-start | bytes 7077888 | tf_op jit(solution)/shard_map/all_gather | solution.py:173
  9.6 1.5 copy-start.3
  9.7 149.8 %all-gather.6.cloned.1.call-start = ((), (), s32[]{:S(2)}) async-start(), calls=%async_computation.4 | async-start | bytes 7077888 | tf_op jit(solution)/shard_map/all_gather | solution.py:173
  10.4 157.1 %all-gather.8.cloned.1.call-start = ((), (), s32[]{:S(2)}) async-start(), calls=%async_computation.5 | async-start | bytes 7077888 | tf_op jit(solution)/shard_map/all_gather | solution.py:173
  12.6 28.8 %copy-start.2 = (bf16[1536,384]{1,0:T(8,128)(2,1)S(1)}, bf16[1536,384]{1,0:T(8,128)(2,1)}, u32[]{:S(2)}) copy-start(bf16[1536,384]{1,0:T(8,128)(2,1)} %param.7) | copy-start | bytes 3538948
  12.8 15.8 %collective-permute-start.16 = (bf16[1536,256]{1,0:T(8,128)(2,1)S(1)}, bf16[1536,256]{1,0:T(8,128)(2,1)S(1)}, u32[]{:S(2)}, u32[]{:S(2)}) collective-permute-start(bf16[1536,256]{1,0:T(8,128)(2,1)S(1)} %pad_maximum_fusion.2), channel_id=1, source_target_pairs={{0,0},{1,8},{2,2},{3,10},{4,4},{5,12},{6,6},{7,14},{8,1},{9,9},{10... | collective-permute-start | bytes 2359304 | tf_op jit(solution)/shard_map/ppermute | solution.py:148
  19.0 25.5 %copy-start.6 = (s32[4,12]{1,0:T(4,128)S(1)}, s32[4,12]{1,0:T(4,128)}, u32[]{:S(2)}) copy-start(s32[4,12]{1,0:T(4,128)} %param.11) | copy-start | bytes 580
  19.0 50.8 %copy-start.1 = (s32[5]{0:T(128)S(1)}, s32[5]{0:T(128)}, u32[]{:S(2)}) copy-start(s32[5]{0:T(128)} %constant.68.clone) | copy-start | bytes 64
  19.1 18.0 %collective-permute-start.2 = (bf16[1536,256]{1,0:T(8,128)(2,1)S(1)}, bf16[1536,256]{1,0:T(8,128)(2,1)S(1)}, u32[]{:S(2)}, u32[]{:S(2)}) collective-permute-start(bf16[1536,256]{1,0:T(8,128)(2,1)S(1)} %pad_maximum_fusion), channel_id=1, source_target_pairs={{0,0},{1,8},{2,2},{3,10},{4,4},{5,12},{6,6},{7,14},{8,1},{9,9},{10... | collective-permute-start | bytes 2359304 | tf_op jit(solution)/shard_map/ppermute | solution.py:148
  21.1 49.5 %copy-start = (s32[5]{0:T(128)S(1)}, s32[5]{0:T(128)}, u32[]{:S(2)}) copy-start(s32[5]{0:T(128)} %constant.69.clone) | copy-start | bytes 64
  21.1 35.0 %collective-permute-start.9 = (bf16[1536,256]{1,0:T(8,128)(2,1)S(1)}, bf16[1536,256]{1,0:T(8,128)(2,1)S(1)}, u32[]{:S(2)}, u32[]{:S(2)}) collective-permute-start(bf16[1536,256]{1,0:T(8,128)(2,1)S(1)} %pad_maximum_fusion.1), channel_id=1, source_target_pairs={{0,0},{1,8},{2,2},{3,10},{4,4},{5,12},{6,6},{7,14},{8,1},{9,9},{10... | collective-permute-start | bytes 2359304 | tf_op jit(solution)/shard_map/ppermute | solution.py:148
  28.6 35.6 %collective-permute-start.18 = (bf16[1536,256]{1,0:T(8,128)(2,1)S(1)}, bf16[1536,256]{1,0:T(8,128)(2,1)S(1)}, u32[]{:S(2)}, u32[]{:S(2)}) collective-permute-start(bf16[1536,256]{1,0:T(8,128)(2,1)S(1)} %collective-permute-done.16.refs_0_), channel_id=1, source_target_pairs={{1,17},{3,19},{5,21},{7,23},{9,25},{11,27},{13,29},{15,31},{16,0},... | collective-permute-start | bytes 2359304 | tf_op jit(solution)/shard_map/ppermute | solution.py:148
  37.1 28.4 %collective-permute-start.4 = (bf16[1536,256]{1,0:T(8,128)(2,1)S(1)}, bf16[1536,256]{1,0:T(8,128)(2,1)}, u32[]{:S(2)}, u32[]{:S(2)}) collective-permute-start(bf16[1536,256]{1,0:T(8,128)(2,1)S(1)} %collective-permute-done.2.refs_0_), channel_id=1, source_target_pairs={{1,17},{3,19},{5,21},{7,23},{9,25},{11,27},{13,29},{15,31},{16,0},... | collective-permute-start | bytes 2359304 | tf_op jit(solution)/shard_map/ppermute | solution.py:148
  42.6 17.8 %collective-permute-start.8 = (bf16[1536,128]{1,0:T(8,128)(2,1)S(1)}, bf16[1536,128]{1,0:T(8,128)(2,1)S(1)}, u32[]{:S(2)}, u32[]{:S(2)}) collective-permute-start(bf16[1536,128]{1,0:T(8,128)(2,1)S(1)} %get-tuple-element.16), channel_id=1, source_target_pairs={{0,0},{1,8},{2,2},{3,10},{4,4},{5,12},{6,6},{7,14},{8,1},{9,9},{10... | collective-permute-start | bytes 1179656 | tf_op jit(solution)/shard_map/ppermute | solution.py:148
  44.6 8.7 %collective-permute-start = (s32[4,12]{1,0:T(4,128)S(1)}, s32[4,12]{1,0:T(4,128)S(1)}, u32[]{:S(2)}, u32[]{:S(2)}) collective-permute-start(s32[4,12]{1,0:T(4,128)S(1)} %copy-done.6), channel_id=1, source_target_pairs={{0,0},{1,8},{2,2},{3,10},{4,4},{5,12},{6,6},{7,14},{8,1},{9,9},{10... | collective-permute-start | bytes 584 | tf_op jit(solution)/shard_map/ppermute | solution.py:148
  53.2 15.3 %copy-start.5 = (s32[4,12]{1,0:T(4,128)}, s32[4,12]{1,0:T(4,128)S(1)}, u32[]{:S(2)}) copy-start(s32[4,12]{1,0:T(4,128)S(1)} %collective-permute-done) | copy-start | bytes 580
  53.2 10.9 %collective-permute-start.1 = (bf16[1536,128]{1,0:T(8,128)(2,1)}, bf16[1536,128]{1,0:T(8,128)(2,1)}, u32[]{:S(2)}, u32[]{:S(2)}) collective-permute-start(bf16[1536,128]{1,0:T(8,128)(2,1)} %get-tuple-element.15), channel_id=1, source_target_pairs={{0,0},{1,8},{2,2},{3,10},{4,4},{5,12},{6,6},{7,14},{8,1},{9,9},{10... | collective-permute-start | bytes 1179656 | tf_op jit(solution)/shard_map/ppermute | solution.py:148
  56.1 15.4 %collective-permute-start.11 = (bf16[1536,256]{1,0:T(8,128)(2,1)S(1)}, bf16[1536,256]{1,0:T(8,128)(2,1)}, u32[]{:S(2)}, u32[]{:S(2)}) collective-permute-start(bf16[1536,256]{1,0:T(8,128)(2,1)S(1)} %collective-permute-done.9.refs_0_), channel_id=1, source_target_pairs={{1,17},{3,19},{5,21},{7,23},{9,25},{11,27},{13,29},{15,31},{16,0},... | collective-permute-start | bytes 2359304 | tf_op jit(solution)/shard_map/ppermute | solution.py:148
  60.4 12.4 %collective-permute-start.10 = (bf16[1536,256]{1,0:T(8,128)(2,1)S(1)}, bf16[1536,256]{1,0:T(8,128)(2,1)}, u32[]{:S(2)}, u32[]{:S(2)}) collective-permute-start(bf16[1536,256]{1,0:T(8,128)(2,1)S(1)} %collective-permute-done.9.refs_0_), channel_id=1, source_target_pairs={{0,1},{1,0},{2,3},{3,2},{4,5},{5,4},{6,7},{7,6},{8,9},{9,8},{10,11... | collective-permute-start | bytes 2359304 | tf_op jit(solution)/shard_map/ppermute | solution.py:148
  64.1 11.2 %collective-permute-start.3 = (bf16[1536,256]{1,0:T(8,128)(2,1)S(1)}, bf16[1536,256]{1,0:T(8,128)(2,1)}, u32[]{:S(2)}, u32[]{:S(2)}) collective-permute-start(bf16[1536,256]{1,0:T(8,128)(2,1)S(1)} %collective-permute-done.2.refs_0_), channel_id=1, source_target_pairs={{0,1},{1,0},{2,3},{3,2},{4,5},{5,4},{6,7},{7,6},{8,9},{9,8},{10,11... | collective-permute-start | bytes 2359304 | tf_op jit(solution)/shard_map/ppermute | solution.py:148
  64.1 13.1 %collective-permute-start.6 = (bf16[1536,256]{1,0:T(8,128)(2,1)S(1)}, bf16[1536,256]{1,0:T(8,128)(2,1)}, u32[]{:S(2)}, u32[]{:S(2)}) collective-permute-start(bf16[1536,256]{1,0:T(8,128)(2,1)S(1)} %collective-permute-done.2.refs_0_), channel_id=1, source_target_pairs={{0,16},{2,18},{4,20},{6,22},{8,24},{10,26},{12,28},{14,30},{16,32}... | collective-permute-start | bytes 2359304 | tf_op jit(solution)/shard_map/ppermute | solution.py:148
  65.4 13.1 %collective-permute-start.5 = (bf16[1536,256]{1,0:T(8,128)(2,1)}, bf16[1536,256]{1,0:T(8,128)(2,1)}, u32[]{:S(2)}, u32[]{:S(2)}) collective-permute-start(bf16[1536,256]{1,0:T(8,128)(2,1)} %collective-permute-done.4.refs_2_), channel_id=1, source_target_pairs={{0,1},{1,0},{2,3},{3,2},{4,5},{5,4},{6,7},{7,6},{8,9},{9,8},{10,11... | collective-permute-start | bytes 2359304 | tf_op jit(solution)/shard_map/ppermute | solution.py:148
  71.5 25.2 %collective-permute-start.13 = (bf16[1536,256]{1,0:T(8,128)(2,1)S(1)}, bf16[1536,256]{1,0:T(8,128)(2,1)S(1)}, u32[]{:S(2)}, u32[]{:S(2)}) collective-permute-start(bf16[1536,256]{1,0:T(8,128)(2,1)S(1)} %collective-permute-done.9.refs_0_), channel_id=1, source_target_pairs={{0,16},{2,18},{4,20},{6,22},{8,24},{10,26},{12,28},{14,30},{16,32}... | collective-permute-start | bytes 2359304 | tf_op jit(solution)/shard_map/ppermute | solution.py:148
  72.8 27.8 %collective-permute-start.12 = (bf16[1536,256]{1,0:T(8,128)(2,1)}, bf16[1536,256]{1,0:T(8,128)(2,1)S(1)}, u32[]{:S(2)}, u32[]{:S(2)}) collective-permute-start(bf16[1536,256]{1,0:T(8,128)(2,1)} %collective-permute-done.11.refs_2_), channel_id=1, source_target_pairs={{0,1},{1,0},{2,3},{3,2},{4,5},{5,4},{6,7},{7,6},{8,9},{9,8},{10,11... | collective-permute-start | bytes 2359304 | tf_op jit(solution)/shard_map/ppermute | solution.py:148
  75.4 50.1 %collective-permute-start.17 = (bf16[1536,256]{1,0:T(8,128)(2,1)S(1)}, bf16[1536,256]{1,0:T(8,128)(2,1)}, u32[]{:S(2)}, u32[]{:S(2)}) collective-permute-start(bf16[1536,256]{1,0:T(8,128)(2,1)S(1)} %collective-permute-done.16.refs_0_), channel_id=1, source_target_pairs={{0,1},{1,0},{2,3},{3,2},{4,5},{5,4},{6,7},{7,6},{8,9},{9,8},{10,11... | collective-permute-start | bytes 2359304 | tf_op jit(solution)/shard_map/ppermute | solution.py:148
  77.3 48.2 %collective-permute-start.20 = (bf16[1536,256]{1,0:T(8,128)(2,1)S(1)}, bf16[1536,256]{1,0:T(8,128)(2,1)}, u32[]{:S(2)}, u32[]{:S(2)}) collective-permute-start(bf16[1536,256]{1,0:T(8,128)(2,1)S(1)} %collective-permute-done.16.refs_0_), channel_id=1, source_target_pairs={{0,16},{2,18},{4,20},{6,22},{8,24},{10,26},{12,28},{14,30},{16,32}... | collective-permute-start | bytes 2359304 | tf_op jit(solution)/shard_map/ppermute | solution.py:148
  78.6 46.9 %collective-permute-start.19 = (bf16[1536,256]{1,0:T(8,128)(2,1)S(1)}, bf16[1536,256]{1,0:T(8,128)(2,1)}, u32[]{:S(2)}, u32[]{:S(2)}) collective-permute-start(bf16[1536,256]{1,0:T(8,128)(2,1)S(1)} %collective-permute-done.18.refs_2_), channel_id=1, source_target_pairs={{0,1},{1,0},{2,3},{3,2},{4,5},{5,4},{6,7},{7,6},{8,9},{9,8},{10,11... | collective-permute-start | bytes 2359304 | tf_op jit(solution)/shard_map/ppermute | solution.py:148
  96.7 28.7 %collective-permute-start.15 = (bf16[1536,128]{1,0:T(8,128)(2,1)}, bf16[1536,128]{1,0:T(8,128)(2,1)S(1)}, u32[]{:S(2)}, u32[]{:S(2)}) collective-permute-start(bf16[1536,128]{1,0:T(8,128)(2,1)} %get-tuple-element.14), channel_id=1, source_target_pairs={{0,0},{1,8},{2,2},{3,10},{4,4},{5,12},{6,6},{7,14},{8,1},{9,9},{10... | collective-permute-start | bytes 1179656 | tf_op jit(solution)/shard_map/ppermute | solution.py:148
  100.6 16.6 %collective-permute-start.7 = (bf16[1536,128]{1,0:T(8,128)(2,1)S(1)}, bf16[1536,128]{1,0:T(8,128)(2,1)S(1)}, u32[]{:S(2)}, u32[]{:S(2)}) collective-permute-start(bf16[1536,128]{1,0:T(8,128)(2,1)S(1)} %shard_map.73), channel_id=1, source_target_pairs={{0,0},{1,8},{2,2},{3,10},{4,4},{5,12},{6,6},{7,14},{8,1},{9,9},{10... | collective-permute-start | bytes 1179656 | tf_op jit(solution)/shard_map/ppermute | solution.py:148
  117.2 3.8 %copy-start.4 = (bf16[1536,128]{1,0:T(8,128)(2,1)}, bf16[1536,128]{1,0:T(8,128)(2,1)S(1)}, u32[]{:S(2)}) copy-start(bf16[1536,128]{1,0:T(8,128)(2,1)S(1)} %collective-permute-done.7) | copy-start | bytes 1179652
  117.2 25.0 %collective-permute-start.14 = (bf16[1536,128]{1,0:T(8,128)(2,1)S(1)}, bf16[1536,128]{1,0:T(8,128)(2,1)}, u32[]{:S(2)}, u32[]{:S(2)}) collective-permute-start(bf16[1536,128]{1,0:T(8,128)(2,1)S(1)} %shard_map.74), channel_id=1, source_target_pairs={{0,0},{1,8},{2,2},{3,10},{4,4},{5,12},{6,6},{7,14},{8,1},{9,9},{10... | collective-permute-start | bytes 1179656 | tf_op jit(solution)/shard_map/ppermute | solution.py:148
  121.0 21.2 %all-to-all-start = ((bf16[8,192,128]{2,1,0:T(8,128)(2,1)}), bf16[8,192,128]{2,1,0:T(8,128)(2,1)S(1)}, u32[]{:S(2)}, u32[]{:S(2)}) async-start(bf16[8,192,128]{2,1,0:T(8,128)(2,1)} %bitcast.30), calls=%async_computation | async-start | bytes 786432 | tf_op jit(solution)/shard_map/all_to_all | solution.py:172
  138.9 14.0 %collective-permute-start.21 = (bf16[1536,128]{1,0:T(8,128)(2,1)S(1)}, bf16[1536,128]{1,0:T(8,128)(2,1)}, u32[]{:S(2)}, u32[]{:S(2)}) collective-permute-start(bf16[1536,128]{1,0:T(8,128)(2,1)S(1)} %shard_map.75), channel_id=1, source_target_pairs={{0,0},{1,8},{2,2},{3,10},{4,4},{5,12},{6,6},{7,14},{8,1},{9,9},{10... | collective-permute-start | bytes 1179656 | tf_op jit(solution)/shard_map/ppermute | solution.py:148
  142.2 13.0 %all-to-all-start.1 = ((bf16[8,192,128]{2,1,0:T(8,128)(2,1)}), bf16[8,192,128]{2,1,0:T(8,128)(2,1)S(1)}, u32[]{:S(2)}, u32[]{:S(2)}) async-start(bf16[8,192,128]{2,1,0:T(8,128)(2,1)} %bitcast.2), calls=%async_computation.1 | async-start | bytes 786432 | tf_op jit(solution)/shard_map/all_to_all | solution.py:172
  155.2 12.3 %all-to-all-start.2 = ((bf16[8,192,128]{2,1,0:T(8,128)(2,1)}), bf16[8,192,128]{2,1,0:T(8,128)(2,1)S(1)}, u32[]{:S(2)}, u32[]{:S(2)}) async-start(bf16[8,192,128]{2,1,0:T(8,128)(2,1)} %bitcast.4), calls=%async_computation.2 | async-start | bytes 786432 | tf_op jit(solution)/shard_map/all_to_all | solution.py:172
Sparse Core Ops, SparseCore 0:
  9.8 47.7 all-gather.3
  59.3 43.5 all-gather.5
  104.8 47.8 all-gather.7

commit v2 on v1

v2 whole, which is shorter than its diff:
```python
import functools
import math

import jax
import jax.numpy as jnp
from jax import lax
from jax.experimental import pallas as pl
from jax.experimental.pallas import tpu as pltpu
from jax.sharding import PartitionSpec as P

HD = 128
TILE = 384
CHUNK = 192
JOINED = 6
SCALE = math.log2(math.e) / math.sqrt(HD)
PROJ_FLOPS = 3_000_000_000
PLACE = ("frame", "head")
ATT_FLOPS = 10_000_000_000


def attend_kernel(first, ids, inner, query, own, other, *refs):
    inner_slabs, outer_slabs = refs[0:3], refs[3:6]
    o_ref, q_ref, key_bank, value_bank, even, odd, sems = refs[6:]
    tokens = o_ref.shape[0]
    heads = key_bank.shape[0]
    width = own.shape[1] // 2

    def transfer(kind, head, then):
        at = kind * width + (first + head) * HD

        def copy(i, ref):
            rows = pl.ds(i * tokens, tokens)
            bank = (key_bank.at[head, rows, :], value_bank.at[head, rows, 0:HD])[kind]
            moved = pltpu.make_async_copy(
                ref.at[:, at : at + HD], bank, sems.at[head, 2 * i + kind]
            )
            getattr(moved, then)()

        copy(0, own)
        copy(1, other)

        @pl.when(inner[0] == 1)
        def _():
            for i in range(3):
                copy(2 + i, inner_slabs[i])

        @pl.when(inner[0] == 0)
        def _():
            for i in range(3):
                copy(2 + i, outer_slabs[i])

    asked = pltpu.make_async_copy(
        query.at[pl.ds(0, tokens), first * HD : (first + heads) * HD], q_ref, sems.at[0, 10]
    )
    asked.start()
    for head in range(heads):
        transfer(0, head, "start")
        transfer(1, head, "start")
    for head in range(heads):
        value_bank[head, :, HD : 2 * HD] = jnp.ones((5 * tokens, HD), jnp.bfloat16)
    asked.wait()
    for head in range(heads):
        cols = slice(head * HD, (head + 1) * HD)
        attend_head(
            ids,
            q_ref.at[:, cols],
            key_bank.at[head],
            value_bank.at[head],
            o_ref.at[:, cols],
            even,
            odd,
            functools.partial(transfer, head=head, then="wait"),
        )


def attend_head(ids, q_ref, key_bank, value_bank, o_ref, even, odd, ready):
    listed = ids.shape[1]
    chunks = o_ref.shape[0] // CHUNK

    def tile_rows(chunk, j):
        return pl.ds(pl.multiple_of(ids[chunk * CHUNK // TILE, j] * TILE, TILE), TILE)

    def chunk_rows(chunk):
        return pl.ds(pl.multiple_of(chunk * CHUNK, CHUNK), CHUNK)

    def score(chunk, store, j):
        tile_scores = lax.dot_general(
            q_ref[chunk_rows(chunk), :],
            key_bank[tile_rows(chunk, j), :],
            (((1,), (1,)), ((), ())),
            preferred_element_type=jnp.float32,
        )
        store[:, j * TILE : (j + 1) * TILE] = tile_scores
        return functools.reduce(
            jnp.maximum, [tile_scores[:, i : i + HD] for i in range(0, TILE, HD)]
        )

    def weigh(chunk, store, j, row_max):
        weights = jnp.exp2(store[:, j * TILE : (j + JOINED) * TILE] * SCALE - row_max)
        tiles = [value_bank[tile_rows(chunk, j + i), :] for i in range(JOINED)]
        return jnp.dot(
            weights.astype(jnp.bfloat16),
            jnp.concatenate(tiles, axis=0),
            preferred_element_type=jnp.float32,
        )

    def finish(chunk, total):
        o_ref[chunk_rows(chunk), :] = (total[:, 0:HD] / total[:, HD : 2 * HD]).astype(jnp.bfloat16)

    def row_limit(lane_max):
        return jnp.max(lane_max, axis=1, keepdims=True) * SCALE

    def both(chunk, now, later, row_max):
        lane_max, total = None, None
        for j in range(listed):
            found = score(chunk + 1, later, j)
            lane_max = found if lane_max is None else jnp.maximum(lane_max, found)
            if (j + 1) % JOINED == 0:
                term = weigh(chunk, now, j + 1 - JOINED, row_max)
                total = term if total is None else total + term
        finish(chunk, total)
        return row_limit(lane_max)

    def pair(step, row_max):
        row_max = both(2 * step, even, odd, row_max)
        return both(2 * step + 1, odd, even, row_max)

    ready(0)
    row_max = row_limit(
        functools.reduce(jnp.maximum, [score(0, even, j) for j in range(listed)])
    )
    ready(1)
    row_max = lax.fori_loop(0, chunks // 2 - 1, pair, row_max)
    row_max = both(chunks - 2, even, odd, row_max)
    total = functools.reduce(
        jnp.add, [weigh(chunks - 1, odd, j, row_max) for j in range(0, listed, JOINED)]
    )
    finish(chunks - 1, total)


def attend(ids, inner, first, heads, arrays):
    tokens = arrays[1].shape[0]
    listed = ids.shape[1]
    anywhere = pl.BlockSpec(memory_space=pl.ANY)
    in_smem = pl.BlockSpec(memory_space=pltpu.MemorySpace.SMEM)
    return pl.pallas_call(
        functools.partial(attend_kernel, first),
        out_shape=jax.ShapeDtypeStruct((tokens, heads * HD), jnp.bfloat16),
        in_specs=[in_smem, in_smem] + [anywhere] * len(arrays),
        out_specs=pl.BlockSpec(memory_space=pltpu.MemorySpace.VMEM),
        scratch_shapes=[
            pltpu.VMEM((tokens, heads * HD), jnp.bfloat16),
            pltpu.VMEM((heads, 5 * tokens, HD), jnp.bfloat16),
            pltpu.VMEM((heads, 5 * tokens, 2 * HD), jnp.bfloat16),
            pltpu.VMEM((CHUNK, listed * TILE), jnp.float32),
            pltpu.VMEM((CHUNK, listed * TILE), jnp.float32),
            pltpu.SemaphoreType.DMA((heads, 11)),
        ],
        compiler_params=pltpu.CompilerParams(vmem_limit_bytes=56 * 1024 * 1024),
        cost_estimate=pl.CostEstimate(
            flops=heads * ATT_FLOPS, bytes_accessed=1024, transcendentals=0
        ),
        name="attend",
    )(ids, inner, *arrays)


def project_kernel(rows, weight, *refs):
    out, packed = refs[-2], refs[-1]
    groups, _, width = rows.shape

    @pl.when(pl.program_id(0) == 0)
    def _():
        for g in range(groups):
            packed[:, g * width : (g + 1) * width] = rows[g]

    total = jnp.dot(
        packed[...],
        weight[...].reshape(groups * width, weight.shape[-1]),
        preferred_element_type=jnp.float32,
    )
    if len(refs) > 2:
        total = total + refs[0][...]
    out[...] = total.astype(out.dtype)


def project(rows, weight, place, earlier):
    groups, tokens, width = rows.shape
    columns = weight.shape[-1]
    step = 1024
    part = pl.BlockSpec((tokens, step), lambda i: (0, i))
    return pl.pallas_call(
        project_kernel,
        out_shape=jax.ShapeDtypeStruct(
            (tokens, columns), jnp.float32 if earlier is None else jnp.bfloat16
        ),
        grid=(columns // step,),
        in_specs=[
            pl.BlockSpec((groups, tokens, width), lambda i: (0, 0, 0)),
            pl.BlockSpec((groups, width, step), lambda i: (0, place, i)),
        ]
        + ([] if earlier is None else [part]),
        out_specs=part,
        scratch_shapes=[pltpu.VMEM((tokens, groups * width), jnp.bfloat16)],
        compiler_params=pltpu.CompilerParams(vmem_limit_bytes=56 * 1024 * 1024),
        cost_estimate=pl.CostEstimate(flops=PROJ_FLOPS, bytes_accessed=1024, transcendentals=0),
        name="project",
    )(rows, weight, *([] if earlier is None else [earlier]))


def after(value, *earlier):
    return lax.optimization_barrier((value, *earlier))[0]


def on_device(query, keys, values, out_weight, tile_lists):
    frames = lax.axis_size("frame")
    groups = lax.axis_size("head")
    heads_here = query.shape[1] // HD
    tokens = query.shape[0]
    tiles_here = tokens // TILE
    frame = lax.axis_index("frame")
    head = lax.axis_index("head")

    def route(target, chosen=lambda a, c: True):
        pairs = []
        for z in range(frames // 2):
            for a in range(2):
                for y in range(groups // 2):
                    for c in range(2):
                        z2, a2, c2 = target(z, a, c)
                        if 0 <= z2 < frames // 2 and chosen(a, c):
                            source = (2 * z + a) * groups + 2 * y + c
                            pairs.append((source, (2 * z2 + a2) * groups + 2 * y + c2))
        return pairs

    def is_inner(a, c):
        return a == c

    def is_outer(a, c):
        return a != c

    def to_near(z, a, c):
        return z - 1 if c == 0 else z + 1, a, c

    def to_far(z, a, c):
        return z + 1 if c == 0 else z - 1, a, c

    def to_core(z, a, c):
        return z, a, 1 - c

    turn = route(lambda z, a, c: (z, c, a))
    swap = route(to_core)

    def move(block, pairs):
        return lax.ppermute(block, PLACE, pairs)

    weight = lax.all_gather(out_weight, "head", axis=0, tiled=True)
    weight = weight.reshape(groups, heads_here * HD, out_weight.shape[1])

    pair = jnp.concatenate([keys, values], axis=1)
    own = move(pair, turn)
    inner_near = move(pair, route(to_near, is_inner))
    inner_far = move(pair, route(to_far, is_inner))
    noted = jnp.pad(
        tile_lists.astype(jnp.bfloat16),
        ((0, 16 - tiles_here), (0, query.shape[1] - tile_lists.shape[1])),
    )
    asked = jnp.concatenate([query, noted], axis=0)
    ready = after(own, inner_near, inner_far)
    near = move(ready, route(to_near, is_outer))
    far = move(ready, route(to_far, is_outer))
    other = move(own, swap)
    asked = move(after(asked, other), turn)
    inner_crossed = move(inner_near, route(to_core, is_inner))
    crossed = move(after(near, asked), route(to_core, is_outer))

    core = head % 2
    slab = frame // 2 * 2 + core
    inner = (frame % 2 == core).astype(jnp.int32).reshape(1)
    lists = asked[tokens : tokens + tiles_here, 0 : tile_lists.shape[1]].astype(jnp.int32)
    offset = lists // tiles_here - slab
    side = jnp.where(core == 0, offset, -offset)
    place = jnp.where(side == -2, 4, jnp.where(side == -1, 3, jnp.where(side == 0, 0, side)))
    ids = place * tiles_here + lists % tiles_here

    arrays = [asked, own, other, inner_near, crossed, inner_far, near, inner_crossed, far]
    early = attend(ids, inner, 0, 2, arrays)
    late = attend(after(ids, early), inner, 2, 1, arrays)

    def deliver(attended, width):
        return lax.all_to_all(
            attended.reshape(groups, -1, width * HD), "head", 0, 0, tiled=True
        )

    rows_early = deliver(after(move(early, turn), late), 2)
    rows_late = deliver(move(late, turn), 1)
    first = project(rows_early, weight, 0, None)
    return project(rows_late, weight, 2, first)


def solution(mesh):
    return jax.shard_map(
        on_device,
        mesh=mesh,
        in_specs=(
            P(("video", "frame"), "head"),
            P(("video", "frame"), "head"),
            P(("video", "frame"), "head"),
            P("head", None),
            P(("video", "frame"), None),
        ),
        out_specs=P(("video", "frame", "head"), None),
        check_vma=False,
    )
```

time: 182 us -> 166 us (0.912)
  starting transfers between devices: 76.4 us -> 41.9 us
  waiting for transfers between devices: 21.9 us -> 54.6 us
  matrix products: 17.9 us -> 0 us
  Pallas kernels: 40.7 us -> 49.3 us
  local copies, waits for them, and re-layouts: 7.99 us -> 3.34 us
    ppermute x22 -> x11, waiting for transfers between devices: 16.4 us -> 53.8 us  [move(): return lax.ppermute(block, PLACE, pairs)]
    ppermute x22 -> x11, starting transfers between devices: 62.8 us -> 32 us  [move(): return lax.ppermute(block, PLACE, pairs)]
    dot_general x3 -> x0, matrix products: 17.9 us -> none  [on_device(): term = jnp.dot(rows, weight, preferred_element_type=jnp.float32)]
    pallas_call x3 -> x4, Pallas kernels: 40.7 us -> 49.3 us  [the longest x2 35 us: attend(): pl.pallas_call(functools.partial(attend_kernel, first), out_shape=jax.Sha...]
    slice x3 -> x0, local copies, waits for them, and re-layouts: 5.67 us -> none  [the longest x1 3.09 us: on_device(): weight = lax.all_gather(out_weight[cols, :], 'head', axis=0, tiled=True)]
    all_to_all x3 -> x2, waiting for transfers between devices: 4.13 us -> 0.07 us  [deliver(): lax.all_to_all(attended.reshape(groups, -1, width * HD), 'head', 0, 0, ti...]
    all_to_all x3 -> x2, starting transfers between devices: 13.5 us -> 9.9 us  [deliver(): lax.all_to_all(attended.reshape(groups, -1, width * HD), 'head', 0, 0, ti...]
    unnamed x14 -> x21, local copies, waits for them, and re-layouts: 0.04 us -> 3.11 us
  transfers between devices with their start and end apart: 28 -> 14, of which waited for: 7 -> 5; matrix products, arithmetic and copies ran while one was open for 10% -> 1% of each run, Pallas kernels for 23% -> 26%
where the time goes in v2:
time: 166 us; the launch traced here: 163 us
  waiting for transfers between devices  54.6 us (33%)
  Pallas kernels  49.3 us (30%)
  starting transfers between devices  41.9 us (25%)
  between operations  13.5 us (8%)
  local copies, waits for them, and re-layouts  3.34 us (2%)
    ppermute x11, waiting for transfers between devices, move(): return lax.ppermute(block, PLACE, pairs)  53.8 us
    pallas_call x2, Pallas kernels, attend(): pl.pallas_call(functools.partial(attend_kernel, first), out_shape=jax.Sha...  35 us
    ppermute x11, starting transfers between devices, move(): return lax.ppermute(block, PLACE, pairs)  32 us
    pallas_call x2, Pallas kernels, project(): pl.pallas_call(project_kernel, out_shape=jax.ShapeDtypeStruct((tokens, co...  14.3 us
    all_to_all x2, starting transfers between devices, deliver(): lax.all_to_all(attended.reshape(groups, -1, width * HD), 'head', 0, 0, ti...  9.9 us
  transfers between devices with their start and end apart: 14, of which 5 were waited for; matrix products, arithmetic and copies ran while one was open for 1% of the time, Pallas kernels for 26%

profile of v2, /device:TPU:1, one launch (start us, length us, event | category | flops | bytes accessed | tf_op | source)
XLA Modules:
  0.0 163.4 jit_solution(12568252038521082975)
XLA Ops:
  6.5 0.0 copy-start.2
  6.5 0.0 copy-start.3
  6.5 0.0 all-gather.2.cloned.1.call-start
  6.5 0.7 all-gather.2.cloned.1.call-update
  7.3 0.5 copy-done.2
  7.8 0.0 copy-start.5
  7.8 0.0 copy-start.4
  7.8 0.1 constant_dynamic-update-slice_fusion.1
  7.9 0.2 copy-done.3
  8.2 0.2 constant_dynamic-update-slice_fusion
  8.4 6.0 %collective-permute-start = (bf16[1536,768]{1,0:T(8,128)(2,1)S(1)}, bf16[1536,768]{1,0:T(8,128)(2,1)S(1)}, u32[]{:S(2)}, u32[]{:S(2)}) collective-permute-start(bf16[1536,768]{1,0:T(8,128)(2,1)S(1)} %constant_dynamic-update-slice_fusion), channel_id=1, source_target_pairs={{0,0},{1,8},{2,2},{3,10},{4,4},{5,12},{6,6},{7,14},{8,1},{9,9},{10... | collective-permute-start | bytes 7077896 | tf_op jit(solution)/shard_map/ppermute | solution.py:254
  14.5 2.1 %collective-permute-start.3 = (bf16[1536,768]{1,0:T(8,128)(2,1)S(1)}, bf16[1536,768]{1,0:T(8,128)(2,1)}, u32[]{:S(2)}, u32[]{:S(2)}) collective-permute-start(bf16[1536,768]{1,0:T(8,128)(2,1)S(1)} %constant_dynamic-update-slice_fusion), channel_id=1, source_target_pairs={{9,25},{11,27},{13,29},{15,31},{16,0},{18,2},{20,4},{22,6},{25,41}... | collective-permute-start | bytes 7077896 | tf_op jit(solution)/shard_map/ppermute | solution.py:254
  16.6 0.8 collective-permute-start.4
  17.4 23.6 %collective-permute-done.own = bf16[1536,768]{1,0:T(8,128)(2,1)S(1)} collective-permute-done((bf16[1536,768]{1,0:T(8,128)(2,1)S(1)}, bf16[1536,768]{1,0:T(8,128)(2,1)S(1)}, u32[]{:S(2)}, u32[]{:S(2)}) %collective-permute-start) | collective-permute-done | bytes 2359328 | tf_op jit(solution)/shard_map/ppermute | solution.py:254
  41.0 0.0 copy-start.7
  41.0 0.0 collective-permute-start.1
  41.0 0.0 collective-permute-done.3.refs_0_
  41.0 0.0 collective-permute-done.4.refs_2_
  41.0 0.0 copy-start.8
  41.0 1.4 copy-done.8
  42.5 4.9 %collective-permute-start.5 = (bf16[1536,768]{1,0:T(8,128)(2,1)S(1)}, bf16[1536,768]{1,0:T(8,128)(2,1)}, u32[]{:S(2)}, u32[]{:S(2)}) collective-permute-start(bf16[1536,768]{1,0:T(8,128)(2,1)S(1)} %collective-permute-done.own), channel_id=1, source_target_pairs={{1,17},{3,19},{5,21},{7,23},{17,33},{19,35},{21,37},{23,39},{24,8}... | collective-permute-start | bytes 7077896 | tf_op jit(solution)/shard_map/ppermute | solution.py:254
  47.4 0.0 copy-done.5
  47.4 0.0 copy-done.4
  47.4 0.1 fusion.1
  47.5 0.0 collective-permute-done.1.other
  47.5 0.0 copy-start.9
  47.5 3.1 %collective-permute-start.2 = (bf16[1552,384]{1,0:T(8,128)(2,1)S(1)}, bf16[1552,384]{1,0:T(8,128)(2,1)S(1)}, u32[]{:S(2)}, u32[]{:S(2)}) collective-permute-start(bf16[1552,384]{1,0:T(8,128)(2,1)S(1)} %fusion.1), channel_id=1, source_target_pairs={{0,0},{1,8},{2,2},{3,10},{4,4},{5,12},{6,6},{7,14},{8,1},{9,9},{10... | collective-permute-start | bytes 3575816 | tf_op jit(solution)/shard_map/ppermute | solution.py:254
  50.6 1.3 collective-permute-start.8
  51.9 1.3 collective-permute-start.7
  53.2 18.5 %collective-permute-done.5.refs_3_ = bf16[1536,768]{1,0:T(8,128)(2,1)} collective-permute-done((bf16[1536,768]{1,0:T(8,128)(2,1)S(1)}, bf16[1536,768]{1,0:T(8,128)(2,1)}, u32[]{:S(2)}, u32[]{:S(2)}) %collective-permute-start.5) | collective-permute-done | bytes 2359328 | tf_op jit(solution)/shard_map/ppermute | solution.py:254
  71.8 0.0 collective-permute-done.2.query
  71.8 0.0 copy-done.9
  71.8 0.0 copy-start.6
  71.8 2.8 %collective-permute-start.6 = (bf16[1536,768]{1,0:T(8,128)(2,1)}, bf16[1536,768]{1,0:T(8,128)(2,1)}, u32[]{:S(2)}, u32[]{:S(2)}) collective-permute-start(bf16[1536,768]{1,0:T(8,128)(2,1)} %collective-permute-done.5.refs_3_), channel_id=1, source_target_pairs={{1,0},{3,2},{5,4},{7,6},{8,9},{10,11},{12,13},{14,15},{17,16},{19,... | collective-permute-start | bytes 7077896 | tf_op jit(solution)/shard_map/ppermute | solution.py:254
  74.5 0.6 fusion.3.ids
  75.1 5.7 %collective-permute-done.8.refs_5_ = bf16[1536,768]{1,0:T(8,128)(2,1)} collective-permute-done((bf16[1536,768]{1,0:T(8,128)(2,1)S(1)}, bf16[1536,768]{1,0:T(8,128)(2,1)}, u32[]{:S(2)}, u32[]{:S(2)}) %collective-permute-start.8) | collective-permute-done | bytes 2359328 | tf_op jit(solution)/shard_map/ppermute | solution.py:254
  80.8 0.0 collective-permute-done.7.refs_4_
  80.8 0.0 collective-permute-done.6.refs_1_
  80.8 0.0 copy-done.7
  80.8 0.0 copy-done.6
  80.8 22.3 %attend.2 = bf16[1536,256]{1,0:T(8,128)(2,1)} custom-call(s32[4,12]{1,0:T(4,128)} %fusion.3.ids, s32[1]{0:T(128)} %bitcast.inner, bf16[1552,384]{1,0:T(8,128)(2,1)} %copy-done.6, bf16[1536,768]{1,0:T(8,128)(2,1)} %copy-done.7, bf16[1536,768]{1,0:T(8,128)(2,1)} %copy-done.9, bf16[1536,768]{1,0:T(8,128)(2,1)} %collective-permute-done.3.refs_0_, ...), custom_call_target="tpu_custom_call" | custom-call | flops 20000000000 | bytes 1024 | tf_op jit(solution)/shard_map/attend/pallas_call | solution.py:146
  103.1 3.4 %collective-permute-start.10 = (bf16[1536,256]{1,0:T(8,128)(2,1)}, bf16[1536,256]{1,0:T(8,128)(2,1)}, u32[]{:S(2)}, u32[]{:S(2)}) collective-permute-start(bf16[1536,256]{1,0:T(8,128)(2,1)} %attend.2), channel_id=1, source_target_pairs={{0,0},{1,8},{2,2},{3,10},{4,4},{5,12},{6,6},{7,14},{8,1},{9,9},{10... | collective-permute-start | bytes 2359304 | tf_op jit(solution)/shard_map/ppermute | solution.py:254
  106.6 12.7 %attend.3 = bf16[1536,128]{1,0:T(8,128)(2,1)} custom-call(s32[4,12]{1,0:T(4,128)} %fusion.3.ids, s32[1]{0:T(128)} %bitcast.inner, bf16[1552,384]{1,0:T(8,128)(2,1)} %copy-done.6, bf16[1536,768]{1,0:T(8,128)(2,1)} %copy-done.7, bf16[1536,768]{1,0:T(8,128)(2,1)} %copy-done.9, bf16[1536,768]{1,0:T(8,128)(2,1)} %collective-permute-done.3.refs_0_, ...), custom_call_target="tpu_custom_call" | custom-call | flops 10000000000 | bytes 1024 | tf_op jit(solution)/shard_map/attend/pallas_call | solution.py:146
  119.3 0.0 collective-permute-done.10
  119.3 5.2 %all-to-all-start.1 = ((bf16[8,192,256]{2,1,0:T(8,128)(2,1)}), bf16[8,192,256]{2,1,0:T(8,128)(2,1)S(1)}, u32[]{:S(2)}, u32[]{:S(2)}) async-start(bf16[8,192,256]{2,1,0:T(8,128)(2,1)} %bitcast.3), calls=%async_computation.1 | async-start | bytes 1572864 | tf_op jit(solution)/shard_map/all_to_all | solution.py:290
  124.5 6.3 %collective-permute-start.9 = (bf16[1536,128]{1,0:T(8,128)(2,1)}, bf16[1536,128]{1,0:T(8,128)(2,1)}, u32[]{:S(2)}, u32[]{:S(2)}) collective-permute-start(bf16[1536,128]{1,0:T(8,128)(2,1)} %attend.3), channel_id=1, source_target_pairs={{0,0},{1,8},{2,2},{3,10},{4,4},{5,12},{6,6},{7,14},{8,1},{9,9},{10... | collective-permute-start | bytes 1179656 | tf_op jit(solution)/shard_map/ppermute | solution.py:254
  130.8 6.0 %collective-permute-done.9 = bf16[1536,128]{1,0:T(8,128)(2,1)} collective-permute-done((bf16[1536,128]{1,0:T(8,128)(2,1)}, bf16[1536,128]{1,0:T(8,128)(2,1)}, u32[]{:S(2)}, u32[]{:S(2)}) %collective-permute-start.9) | collective-permute-done | bytes 393248 | tf_op jit(solution)/shard_map/ppermute | solution.py:254
  136.7 0.1 all-to-all-done.1.rows
  136.8 0.0 copy-start
  136.8 4.7 %all-to-all-start = ((bf16[8,192,128]{2,1,0:T(8,128)(2,1)}), bf16[8,192,128]{2,1,0:T(8,128)(2,1)S(1)}, u32[]{:S(2)}, u32[]{:S(2)}) async-start(bf16[8,192,128]{2,1,0:T(8,128)(2,1)} %bitcast.1), calls=%async_computation | async-start | bytes 786432 | tf_op jit(solution)/shard_map/all_to_all | solution.py:290
  141.5 0.0 all-gather.2.cloned.1.call-done
  141.5 0.0 copy-done
  141.5 8.3 %project.2.refs_0_ = f32[192,3072]{1,0:T(8,128)} custom-call(bf16[8,192,256]{2,1,0:T(8,128)(2,1)} %copy-done, bf16[8,384,3072]{2,1,0:T(8,128)(2,1)} %bitcast.4), custom_call_target="tpu_custom_call" | custom-call | flops 3000000000 | bytes 1024 | tf_op jit(solution)/shard_map/project/pallas_call | solution.py:191
  149.7 0.0 all-to-all-done.rows
  149.7 0.0 copy-start.1
  149.7 0.8 copy-done.1
  150.5 6.0 %project.3 = bf16[192,3072]{1,0:T(8,128)(2,1)} custom-call(bf16[8,192,128]{2,1,0:T(8,128)(2,1)} %copy-done.1, bf16[8,384,3072]{2,1,0:T(8,128)(2,1)} %bitcast.5, f32[192,3072]{1,0:T(8,128)} %project.2.refs_0_), custom_call_target="tpu_custom_call" | custom-call | flops 3000000000 | bytes 1024 | tf_op jit(solution)/shard_map/project/pallas_call | solution.py:191
  (1 shorter events, 0.0 us)
Async XLA Ops:
  6.5 1.3 copy-start.2
  6.5 1.6 copy-start.3
  6.5 134.9 %all-gather.2.cloned.1.call-start = ((), (), s32[]{:S(2)}) async-start(), calls=%async_computation.2 | async-start | bytes 21233664 | tf_op jit(solution)/shard_map/all_gather | solution.py:256
  7.8 39.6 %copy-start.5 = (s32[4,12]{1,0:T(4,128)S(1)}, s32[4,12]{1,0:T(4,128)}, u32[]{:S(2)}) copy-start(s32[4,12]{1,0:T(4,128)} %param.9) | copy-start | bytes 580
  7.8 39.6 %copy-start.4 = (bf16[1536,384]{1,0:T(8,128)(2,1)S(1)}, bf16[1536,384]{1,0:T(8,128)(2,1)}, u32[]{:S(2)}) copy-start(bf16[1536,384]{1,0:T(8,128)(2,1)} %param.5) | copy-start | bytes 3538948
  8.4 32.6 %collective-permute-start = (bf16[1536,768]{1,0:T(8,128)(2,1)S(1)}, bf16[1536,768]{1,0:T(8,128)(2,1)S(1)}, u32[]{:S(2)}, u32[]{:S(2)}) collective-permute-start(bf16[1536,768]{1,0:T(8,128)(2,1)S(1)} %constant_dynamic-update-slice_fusion), channel_id=1, source_target_pairs={{0,0},{1,8},{2,2},{3,10},{4,4},{5,12},{6,6},{7,14},{8,1},{9,9},{10... | collective-permute-start | bytes 7077896 | tf_op jit(solution)/shard_map/ppermute | solution.py:254
  14.5 26.6 %collective-permute-start.3 = (bf16[1536,768]{1,0:T(8,128)(2,1)S(1)}, bf16[1536,768]{1,0:T(8,128)(2,1)}, u32[]{:S(2)}, u32[]{:S(2)}) collective-permute-start(bf16[1536,768]{1,0:T(8,128)(2,1)S(1)} %constant_dynamic-update-slice_fusion), channel_id=1, source_target_pairs={{9,25},{11,27},{13,29},{15,31},{16,0},{18,2},{20,4},{22,6},{25,41}... | collective-permute-start | bytes 7077896 | tf_op jit(solution)/shard_map/ppermute | solution.py:254
  16.6 24.4 %collective-permute-start.4 = (bf16[1536,768]{1,0:T(8,128)(2,1)S(1)}, bf16[1536,768]{1,0:T(8,128)(2,1)S(1)}, u32[]{:S(2)}, u32[]{:S(2)}) collective-permute-start(bf16[1536,768]{1,0:T(8,128)(2,1)S(1)} %constant_dynamic-update-slice_fusion), channel_id=1, source_target_pairs={{0,16},{2,18},{4,20},{6,22},{16,32},{18,34},{20,36},{22,38},{25,9}... | collective-permute-start | bytes 7077896 | tf_op jit(solution)/shard_map/ppermute | solution.py:254
  41.0 39.8 %copy-start.7 = (bf16[1536,768]{1,0:T(8,128)(2,1)}, bf16[1536,768]{1,0:T(8,128)(2,1)S(1)}, u32[]{:S(2)}) copy-start(bf16[1536,768]{1,0:T(8,128)(2,1)S(1)} %collective-permute-done.own) | copy-start | bytes 7077892
  41.0 6.5 %collective-permute-start.1 = (bf16[1536,768]{1,0:T(8,128)(2,1)S(1)}, bf16[1536,768]{1,0:T(8,128)(2,1)S(1)}, u32[]{:S(2)}, u32[]{:S(2)}) collective-permute-start(bf16[1536,768]{1,0:T(8,128)(2,1)S(1)} %collective-permute-done.own), channel_id=1, source_target_pairs={{0,1},{1,0},{2,3},{3,2},{4,5},{5,4},{6,7},{7,6},{8,9},{9,8},{10,11... | collective-permute-start | bytes 7077896 | tf_op jit(solution)/shard_map/ppermute | solution.py:254
  41.0 1.4 copy-start.8
  42.5 29.3 %collective-permute-start.5 = (bf16[1536,768]{1,0:T(8,128)(2,1)S(1)}, bf16[1536,768]{1,0:T(8,128)(2,1)}, u32[]{:S(2)}, u32[]{:S(2)}) collective-permute-start(bf16[1536,768]{1,0:T(8,128)(2,1)S(1)} %collective-permute-done.own), channel_id=1, source_target_pairs={{1,17},{3,19},{5,21},{7,23},{17,33},{19,35},{21,37},{23,39},{24,8}... | collective-permute-start | bytes 7077896 | tf_op jit(solution)/shard_map/ppermute | solution.py:254
  47.5 24.2 %copy-start.9 = (bf16[1536,768]{1,0:T(8,128)(2,1)}, bf16[1536,768]{1,0:T(8,128)(2,1)S(1)}, u32[]{:S(2)}) copy-start(bf16[1536,768]{1,0:T(8,128)(2,1)S(1)} %collective-permute-done.1.other) | copy-start | bytes 7077892
  47.5 24.2 %collective-permute-start.2 = (bf16[1552,384]{1,0:T(8,128)(2,1)S(1)}, bf16[1552,384]{1,0:T(8,128)(2,1)S(1)}, u32[]{:S(2)}, u32[]{:S(2)}) collective-permute-start(bf16[1552,384]{1,0:T(8,128)(2,1)S(1)} %fusion.1), channel_id=1, source_target_pairs={{0,0},{1,8},{2,2},{3,10},{4,4},{5,12},{6,6},{7,14},{8,1},{9,9},{10... | collective-permute-start | bytes 3575816 | tf_op jit(solution)/shard_map/ppermute | solution.py:254
  50.6 30.2 %collective-permute-start.8 = (bf16[1536,768]{1,0:T(8,128)(2,1)S(1)}, bf16[1536,768]{1,0:T(8,128)(2,1)}, u32[]{:S(2)}, u32[]{:S(2)}) collective-permute-start(bf16[1536,768]{1,0:T(8,128)(2,1)S(1)} %collective-permute-done.own), channel_id=1, source_target_pairs={{8,24},{10,26},{12,28},{14,30},{17,1},{19,3},{21,5},{23,7},{24,40}... | collective-permute-start | bytes 7077896 | tf_op jit(solution)/shard_map/ppermute | solution.py:254
  51.9 28.9 %collective-permute-start.7 = (bf16[1536,768]{1,0:T(8,128)(2,1)}, bf16[1536,768]{1,0:T(8,128)(2,1)}, u32[]{:S(2)}, u32[]{:S(2)}) collective-permute-start(bf16[1536,768]{1,0:T(8,128)(2,1)} %collective-permute-done.3.refs_0_), channel_id=1, source_target_pairs={{0,1},{2,3},{4,5},{6,7},{9,8},{11,10},{13,12},{15,14},{16,17},{18,... | collective-permute-start | bytes 7077896 | tf_op jit(solution)/shard_map/ppermute | solution.py:254
  71.8 9.1 %copy-start.6 = (bf16[1552,384]{1,0:T(8,128)(2,1)}, bf16[1552,384]{1,0:T(8,128)(2,1)S(1)}, u32[]{:S(2)}) copy-start(bf16[1552,384]{1,0:T(8,128)(2,1)S(1)} %collective-permute-done.2.query) | copy-start | bytes 3575812
  71.8 9.0 %collective-permute-start.6 = (bf16[1536,768]{1,0:T(8,128)(2,1)}, bf16[1536,768]{1,0:T(8,128)(2,1)}, u32[]{:S(2)}, u32[]{:S(2)}) collective-permute-start(bf16[1536,768]{1,0:T(8,128)(2,1)} %collective-permute-done.5.refs_3_), channel_id=1, source_target_pairs={{1,0},{3,2},{5,4},{7,6},{8,9},{10,11},{12,13},{14,15},{17,16},{19,... | collective-permute-start | bytes 7077896 | tf_op jit(solution)/shard_map/ppermute | solution.py:254
  103.1 16.1 %collective-permute-start.10 = (bf16[1536,256]{1,0:T(8,128)(2,1)}, bf16[1536,256]{1,0:T(8,128)(2,1)}, u32[]{:S(2)}, u32[]{:S(2)}) collective-permute-start(bf16[1536,256]{1,0:T(8,128)(2,1)} %attend.2), channel_id=1, source_target_pairs={{0,0},{1,8},{2,2},{3,10},{4,4},{5,12},{6,6},{7,14},{8,1},{9,9},{10... | collective-permute-start | bytes 2359304 | tf_op jit(solution)/shard_map/ppermute | solution.py:254
  119.3 17.5 %all-to-all-start.1 = ((bf16[8,192,256]{2,1,0:T(8,128)(2,1)}), bf16[8,192,256]{2,1,0:T(8,128)(2,1)S(1)}, u32[]{:S(2)}, u32[]{:S(2)}) async-start(bf16[8,192,256]{2,1,0:T(8,128)(2,1)} %bitcast.3), calls=%async_computation.1 | async-start | bytes 1572864 | tf_op jit(solution)/shard_map/all_to_all | solution.py:290
  124.5 12.2 %collective-permute-start.9 = (bf16[1536,128]{1,0:T(8,128)(2,1)}, bf16[1536,128]{1,0:T(8,128)(2,1)}, u32[]{:S(2)}, u32[]{:S(2)}) collective-permute-start(bf16[1536,128]{1,0:T(8,128)(2,1)} %attend.3), channel_id=1, source_target_pairs={{0,0},{1,8},{2,2},{3,10},{4,4},{5,12},{6,6},{7,14},{8,1},{9,9},{10... | collective-permute-start | bytes 1179656 | tf_op jit(solution)/shard_map/ppermute | solution.py:254
  136.8 4.7 %copy-start = (bf16[8,192,256]{2,1,0:T(8,128)(2,1)}, bf16[8,192,256]{2,1,0:T(8,128)(2,1)S(1)}, u32[]{:S(2)}) copy-start(bf16[8,192,256]{2,1,0:T(8,128)(2,1)S(1)} %all-to-all-done.1.rows) | copy-start | bytes 2359300
  136.8 12.9 %all-to-all-start = ((bf16[8,192,128]{2,1,0:T(8,128)(2,1)}), bf16[8,192,128]{2,1,0:T(8,128)(2,1)S(1)}, u32[]{:S(2)}, u32[]{:S(2)}) async-start(bf16[8,192,128]{2,1,0:T(8,128)(2,1)} %bitcast.1), calls=%async_computation | async-start | bytes 786432 | tf_op jit(solution)/shard_map/all_to_all | solution.py:290
  149.7 0.8 copy-start.1
Sparse Core Ops, SparseCore 0:
  9.2 100.5 all-gather.1

commit v3 on v2

--- a/solution.py
+++ b/solution.py
@@ -186,7 +186,7 @@
 def project(rows, weight, place, earlier):
     groups, tokens, width = rows.shape
     columns = weight.shape[-1]
-    step = 1024
+    step = 1536
     part = pl.BlockSpec((tokens, step), lambda i: (0, i))
     return pl.pallas_call(
         project_kernel,
@@ -266,7 +266,7 @@
     )
     asked = jnp.concatenate([query, noted], axis=0)
     ready = after(own, inner_near, inner_far)
-    near = move(ready, route(to_near, is_outer))
+    near = move(own, route(to_near, is_outer))
     far = move(ready, route(to_far, is_outer))
     other = move(own, swap)
     asked = move(after(asked, other), turn)

time: 166 us -> 200 us (1.20)
  waiting for transfers between devices: 54.6 us -> 81.4 us
  starting transfers between devices: 41.9 us -> 50.5 us
    ppermute x11, waiting for transfers between devices: 53.8 us -> 79.9 us  [move(): return lax.ppermute(block, PLACE, pairs)]
    ppermute x11, starting transfers between devices: 32 us -> 40.1 us  [move(): return lax.ppermute(block, PLACE, pairs)]
  transfers between devices with their start and end apart: 14 -> 14, of which waited for: 5 -> 5; matrix products, arithmetic and copies ran while one was open for 1% -> 1% of each run, Pallas kernels for 26% -> 22%
where the time goes in v3:
time: 200 us; the launch traced here: 197 us
  waiting for transfers between devices  81.4 us (41%)
  starting transfers between devices  50.5 us (25%)
  Pallas kernels  49.3 us (25%)
  between operations  13.5 us (7%)
    ppermute x11, waiting for transfers between devices, move(): return lax.ppermute(block, PLACE, pairs)  79.9 us
    ppermute x11, starting transfers between devices, move(): return lax.ppermute(block, PLACE, pairs)  40.1 us
    pallas_call x2, Pallas kernels, attend(): pl.pallas_call(functools.partial(attend_kernel, first), out_shape=jax.Sha...  36.7 us
    pallas_call x2, Pallas kernels, project(): pl.pallas_call(project_kernel, out_shape=jax.ShapeDtypeStruct((tokens, co...  12.6 us
    all_to_all x2, starting transfers between devices, deliver(): lax.all_to_all(attended.reshape(groups, -1, width * HD), 'head', 0, 0, ti...  10.4 us
  transfers between devices with their start and end apart: 14, of which 5 were waited for; matrix products, arithmetic and copies ran while one was open for 1% of the time, Pallas kernels for 22%

profile of v3, /device:TPU:1, one launch (start us, length us, event | category | flops | bytes accessed | tf_op | source)
XLA Modules:
  0.0 197.4 jit_solution(13060429925099450682)
XLA Ops:
  6.5 0.0 copy-start.2
  6.5 0.0 copy-start.3
  6.5 0.0 all-gather.2.cloned.1.call-start
  6.5 0.7 all-gather.2.cloned.1.call-update
  7.3 0.5 copy-done.2
  7.8 0.0 copy-start.5
  7.8 0.0 copy-start.4
  7.8 0.1 constant_dynamic-update-slice_fusion.1
  7.9 0.2 copy-done.3
  8.2 0.2 constant_dynamic-update-slice_fusion
  8.4 6.0 %collective-permute-start = (bf16[1536,768]{1,0:T(8,128)(2,1)S(1)}, bf16[1536,768]{1,0:T(8,128)(2,1)S(1)}, u32[]{:S(2)}, u32[]{:S(2)}) collective-permute-start(bf16[1536,768]{1,0:T(8,128)(2,1)S(1)} %constant_dynamic-update-slice_fusion), channel_id=1, source_target_pairs={{0,0},{1,8},{2,2},{3,10},{4,4},{5,12},{6,6},{7,14},{8,1},{9,9},{10... | collective-permute-start | bytes 7077896 | tf_op jit(solution)/shard_map/ppermute | solution.py:254
  14.5 26.6 %collective-permute-done.own = bf16[1536,768]{1,0:T(8,128)(2,1)S(1)} collective-permute-done((bf16[1536,768]{1,0:T(8,128)(2,1)S(1)}, bf16[1536,768]{1,0:T(8,128)(2,1)S(1)}, u32[]{:S(2)}, u32[]{:S(2)}) %collective-permute-start) | collective-permute-done | bytes 2359328 | tf_op jit(solution)/shard_map/ppermute | solution.py:254
  41.0 0.0 copy-start.7
  41.0 0.0 collective-permute-start.1
  41.0 2.2 %collective-permute-start.3 = (bf16[1536,768]{1,0:T(8,128)(2,1)S(1)}, bf16[1536,768]{1,0:T(8,128)(2,1)}, u32[]{:S(2)}, u32[]{:S(2)}) collective-permute-start(bf16[1536,768]{1,0:T(8,128)(2,1)S(1)} %constant_dynamic-update-slice_fusion), channel_id=1, source_target_pairs={{9,25},{11,27},{13,29},{15,31},{16,0},{18,2},{20,4},{22,6},{25,41}... | collective-permute-start | bytes 7077896 | tf_op jit(solution)/shard_map/ppermute | solution.py:254
  43.2 0.8 collective-permute-start.6
  44.0 4.9 %collective-permute-start.4 = (bf16[1536,768]{1,0:T(8,128)(2,1)S(1)}, bf16[1536,768]{1,0:T(8,128)(2,1)}, u32[]{:S(2)}, u32[]{:S(2)}) collective-permute-start(bf16[1536,768]{1,0:T(8,128)(2,1)S(1)} %collective-permute-done.own), channel_id=1, source_target_pairs={{1,17},{3,19},{5,21},{7,23},{17,33},{19,35},{21,37},{23,39},{24,8}... | collective-permute-start | bytes 7077896 | tf_op jit(solution)/shard_map/ppermute | solution.py:254
  49.0 0.0 copy-done.5
  49.0 0.0 copy-done.4
  49.0 0.1 fusion.1
  49.1 0.0 collective-permute-done.1.other
  49.1 0.0 copy-start.8
  49.1 1.9 collective-permute-start.2
  51.0 0.0 collective-permute-done.3.refs_0_
  51.1 0.0 collective-permute-done.6.refs_2_
  51.1 0.0 copy-start.9
  51.1 1.3 collective-permute-start.8
  52.4 1.3 collective-permute-start.7
  53.7 44.9 %collective-permute-done.4.refs_3_ = bf16[1536,768]{1,0:T(8,128)(2,1)} collective-permute-done((bf16[1536,768]{1,0:T(8,128)(2,1)S(1)}, bf16[1536,768]{1,0:T(8,128)(2,1)}, u32[]{:S(2)}, u32[]{:S(2)}) %collective-permute-start.4) | collective-permute-done | bytes 2359328 | tf_op jit(solution)/shard_map/ppermute | solution.py:254
  98.6 0.0 collective-permute-done.2.query
  98.6 0.0 copy-done.8
  98.6 0.0 copy-start.6
  98.6 8.7 %collective-permute-start.5 = (bf16[1536,768]{1,0:T(8,128)(2,1)}, bf16[1536,768]{1,0:T(8,128)(2,1)}, u32[]{:S(2)}, u32[]{:S(2)}) collective-permute-start(bf16[1536,768]{1,0:T(8,128)(2,1)} %collective-permute-done.4.refs_3_), channel_id=1, source_target_pairs={{1,0},{3,2},{5,4},{7,6},{8,9},{10,11},{12,13},{14,15},{17,16},{19,... | collective-permute-start | bytes 7077896 | tf_op jit(solution)/shard_map/ppermute | solution.py:254
  107.3 0.0 copy-done.9
  107.3 0.6 fusion.3.ids
  107.9 0.0 collective-permute-done.8.refs_5_
  107.9 0.0 collective-permute-done.7.refs_4_
  107.9 2.4 %collective-permute-done.5.refs_1_ = bf16[1536,768]{1,0:T(8,128)(2,1)} collective-permute-done((bf16[1536,768]{1,0:T(8,128)(2,1)}, bf16[1536,768]{1,0:T(8,128)(2,1)}, u32[]{:S(2)}, u32[]{:S(2)}) %collective-permute-start.5) | collective-permute-done | bytes 2359328 | tf_op jit(solution)/shard_map/ppermute | solution.py:254
  110.3 0.0 copy-done.7
  110.3 0.0 copy-done.6
  110.3 23.4 %attend.2 = bf16[1536,256]{1,0:T(8,128)(2,1)} custom-call(s32[4,12]{1,0:T(4,128)} %fusion.3.ids, s32[1]{0:T(128)} %bitcast.inner, bf16[1552,384]{1,0:T(8,128)(2,1)} %copy-done.6, bf16[1536,768]{1,0:T(8,128)(2,1)} %copy-done.7, bf16[1536,768]{1,0:T(8,128)(2,1)} %copy-done.8, bf16[1536,768]{1,0:T(8,128)(2,1)} %collective-permute-done.3.refs_0_, ...), custom_call_target="tpu_custom_call" | custom-call | flops 20000000000 | bytes 1024 | tf_op jit(solution)/shard_map/attend/pallas_call | solution.py:146
  133.8 6.6 %collective-permute-start.10 = (bf16[1536,256]{1,0:T(8,128)(2,1)}, bf16[1536,256]{1,0:T(8,128)(2,1)}, u32[]{:S(2)}, u32[]{:S(2)}) collective-permute-start(bf16[1536,256]{1,0:T(8,128)(2,1)} %attend.2), channel_id=1, source_target_pairs={{0,0},{1,8},{2,2},{3,10},{4,4},{5,12},{6,6},{7,14},{8,1},{9,9},{10... | collective-permute-start | bytes 2359304 | tf_op jit(solution)/shard_map/ppermute | solution.py:254
  140.4 13.3 %attend.3 = bf16[1536,128]{1,0:T(8,128)(2,1)} custom-call(s32[4,12]{1,0:T(4,128)} %fusion.3.ids, s32[1]{0:T(128)} %bitcast.inner, bf16[1552,384]{1,0:T(8,128)(2,1)} %copy-done.6, bf16[1536,768]{1,0:T(8,128)(2,1)} %copy-done.7, bf16[1536,768]{1,0:T(8,128)(2,1)} %copy-done.8, bf16[1536,768]{1,0:T(8,128)(2,1)} %collective-permute-done.3.refs_0_, ...), custom_call_target="tpu_custom_call" | custom-call | flops 10000000000 | bytes 1024 | tf_op jit(solution)/shard_map/attend/pallas_call | solution.py:146
  153.7 0.0 collective-permute-done.10
  153.8 5.8 %all-to-all-start.1 = ((bf16[8,192,256]{2,1,0:T(8,128)(2,1)}), bf16[8,192,256]{2,1,0:T(8,128)(2,1)S(1)}, u32[]{:S(2)}, u32[]{:S(2)}) async-start(bf16[8,192,256]{2,1,0:T(8,128)(2,1)} %bitcast.3), calls=%async_computation.1 | async-start | bytes 1572864 | tf_op jit(solution)/shard_map/all_to_all | solution.py:290
  159.5 6.3 %collective-permute-start.9 = (bf16[1536,128]{1,0:T(8,128)(2,1)}, bf16[1536,128]{1,0:T(8,128)(2,1)}, u32[]{:S(2)}, u32[]{:S(2)}) collective-permute-start(bf16[1536,128]{1,0:T(8,128)(2,1)} %attend.3), channel_id=1, source_target_pairs={{0,0},{1,8},{2,2},{3,10},{4,4},{5,12},{6,6},{7,14},{8,1},{9,9},{10... | collective-permute-start | bytes 1179656 | tf_op jit(solution)/shard_map/ppermute | solution.py:254
  165.8 6.0 %collective-permute-done.9 = bf16[1536,128]{1,0:T(8,128)(2,1)} collective-permute-done((bf16[1536,128]{1,0:T(8,128)(2,1)}, bf16[1536,128]{1,0:T(8,128)(2,1)}, u32[]{:S(2)}, u32[]{:S(2)}) %collective-permute-start.9) | collective-permute-done | bytes 393248 | tf_op jit(solution)/shard_map/ppermute | solution.py:254
  171.8 0.0 all-to-all-done.1.rows
  171.8 0.0 copy-start
  171.8 4.7 %all-to-all-start = ((bf16[8,192,128]{2,1,0:T(8,128)(2,1)}), bf16[8,192,128]{2,1,0:T(8,128)(2,1)S(1)}, u32[]{:S(2)}, u32[]{:S(2)}) async-start(bf16[8,192,128]{2,1,0:T(8,128)(2,1)} %bitcast.1), calls=%async_computation | async-start | bytes 786432 | tf_op jit(solution)/shard_map/all_to_all | solution.py:290
  176.5 0.0 all-gather.2.cloned.1.call-done
  176.5 0.0 copy-done
  176.5 7.3 %project.2.refs_0_ = f32[192,3072]{1,0:T(8,128)} custom-call(bf16[8,192,256]{2,1,0:T(8,128)(2,1)} %copy-done, bf16[8,384,3072]{2,1,0:T(8,128)(2,1)} %bitcast.4), custom_call_target="tpu_custom_call" | custom-call | flops 3000000000 | bytes 1024 | tf_op jit(solution)/shard_map/project/pallas_call | solution.py:191
  183.8 0.8 all-to-all-done.rows
  184.6 0.0 copy-start.1
  184.6 0.8 copy-done.1
  185.3 5.3 %project.3 = bf16[192,3072]{1,0:T(8,128)(2,1)} custom-call(bf16[8,192,128]{2,1,0:T(8,128)(2,1)} %copy-done.1, bf16[8,384,3072]{2,1,0:T(8,128)(2,1)} %bitcast.5, f32[192,3072]{1,0:T(8,128)} %project.2.refs_0_), custom_call_target="tpu_custom_call" | custom-call | flops 3000000000 | bytes 1024 | tf_op jit(solution)/shard_map/project/pallas_call | solution.py:191
  (1 shorter events, 0.0 us)
Async XLA Ops:
  6.5 1.3 copy-start.2
  6.5 1.6 copy-start.3
  6.5 170.0 %all-gather.2.cloned.1.call-start = ((), (), s32[]{:S(2)}) async-start(), calls=%async_computation.2 | async-start | bytes 21233664 | tf_op jit(solution)/shard_map/all_gather | solution.py:256
  7.8 41.2 %copy-start.5 = (s32[4,12]{1,0:T(4,128)S(1)}, s32[4,12]{1,0:T(4,128)}, u32[]{:S(2)}) copy-start(s32[4,12]{1,0:T(4,128)} %param.9) | copy-start | bytes 580
  7.8 41.2 %copy-start.4 = (bf16[1536,384]{1,0:T(8,128)(2,1)S(1)}, bf16[1536,384]{1,0:T(8,128)(2,1)}, u32[]{:S(2)}) copy-start(bf16[1536,384]{1,0:T(8,128)(2,1)} %param.5) | copy-start | bytes 3538948
  8.4 32.6 %collective-permute-start = (bf16[1536,768]{1,0:T(8,128)(2,1)S(1)}, bf16[1536,768]{1,0:T(8,128)(2,1)S(1)}, u32[]{:S(2)}, u32[]{:S(2)}) collective-permute-start(bf16[1536,768]{1,0:T(8,128)(2,1)S(1)} %constant_dynamic-update-slice_fusion), channel_id=1, source_target_pairs={{0,0},{1,8},{2,2},{3,10},{4,4},{5,12},{6,6},{7,14},{8,1},{9,9},{10... | collective-permute-start | bytes 7077896 | tf_op jit(solution)/shard_map/ppermute | solution.py:254
  41.0 69.3 %copy-start.7 = (bf16[1536,768]{1,0:T(8,128)(2,1)}, bf16[1536,768]{1,0:T(8,128)(2,1)S(1)}, u32[]{:S(2)}) copy-start(bf16[1536,768]{1,0:T(8,128)(2,1)S(1)} %collective-permute-done.own) | copy-start | bytes 7077892
  41.0 8.1 %collective-permute-start.1 = (bf16[1536,768]{1,0:T(8,128)(2,1)S(1)}, bf16[1536,768]{1,0:T(8,128)(2,1)S(1)}, u32[]{:S(2)}, u32[]{:S(2)}) collective-permute-start(bf16[1536,768]{1,0:T(8,128)(2,1)S(1)} %collective-permute-done.own), channel_id=1, source_target_pairs={{0,1},{1,0},{2,3},{3,2},{4,5},{5,4},{6,7},{7,6},{8,9},{9,8},{10,11... | collective-permute-start | bytes 7077896 | tf_op jit(solution)/shard_map/ppermute | solution.py:254
  41.0 10.0 %collective-permute-start.3 = (bf16[1536,768]{1,0:T(8,128)(2,1)S(1)}, bf16[1536,768]{1,0:T(8,128)(2,1)}, u32[]{:S(2)}, u32[]{:S(2)}) collective-permute-start(bf16[1536,768]{1,0:T(8,128)(2,1)S(1)} %constant_dynamic-update-slice_fusion), channel_id=1, source_target_pairs={{9,25},{11,27},{13,29},{15,31},{16,0},{18,2},{20,4},{22,6},{25,41}... | collective-permute-start | bytes 7077896 | tf_op jit(solution)/shard_map/ppermute | solution.py:254
  43.2 7.8 %collective-permute-start.6 = (bf16[1536,768]{1,0:T(8,128)(2,1)S(1)}, bf16[1536,768]{1,0:T(8,128)(2,1)S(1)}, u32[]{:S(2)}, u32[]{:S(2)}) collective-permute-start(bf16[1536,768]{1,0:T(8,128)(2,1)S(1)} %constant_dynamic-update-slice_fusion), channel_id=1, source_target_pairs={{0,16},{2,18},{4,20},{6,22},{16,32},{18,34},{20,36},{22,38},{25,9}... | collective-permute-start | bytes 7077896 | tf_op jit(solution)/shard_map/ppermute | solution.py:254
  44.0 54.6 %collective-permute-start.4 = (bf16[1536,768]{1,0:T(8,128)(2,1)S(1)}, bf16[1536,768]{1,0:T(8,128)(2,1)}, u32[]{:S(2)}, u32[]{:S(2)}) collective-permute-start(bf16[1536,768]{1,0:T(8,128)(2,1)S(1)} %collective-permute-done.own), channel_id=1, source_target_pairs={{1,17},{3,19},{5,21},{7,23},{17,33},{19,35},{21,37},{23,39},{24,8}... | collective-permute-start | bytes 7077896 | tf_op jit(solution)/shard_map/ppermute | solution.py:254
  49.1 49.5 %copy-start.8 = (bf16[1536,768]{1,0:T(8,128)(2,1)}, bf16[1536,768]{1,0:T(8,128)(2,1)S(1)}, u32[]{:S(2)}) copy-start(bf16[1536,768]{1,0:T(8,128)(2,1)S(1)} %collective-permute-done.1.other) | copy-start | bytes 7077892
  49.1 49.5 %collective-permute-start.2 = (bf16[1552,384]{1,0:T(8,128)(2,1)S(1)}, bf16[1552,384]{1,0:T(8,128)(2,1)S(1)}, u32[]{:S(2)}, u32[]{:S(2)}) collective-permute-start(bf16[1552,384]{1,0:T(8,128)(2,1)S(1)} %fusion.1), channel_id=1, source_target_pairs={{0,0},{1,8},{2,2},{3,10},{4,4},{5,12},{6,6},{7,14},{8,1},{9,9},{10... | collective-permute-start | bytes 3575816 | tf_op jit(solution)/shard_map/ppermute | solution.py:254
  51.1 56.2 %copy-start.9 = (bf16[1536,768]{1,0:T(8,128)(2,1)}, bf16[1536,768]{1,0:T(8,128)(2,1)S(1)}, u32[]{:S(2)}) copy-start(bf16[1536,768]{1,0:T(8,128)(2,1)S(1)} %collective-permute-done.6.refs_2_) | copy-start | bytes 7077892
  51.1 56.8 %collective-permute-start.8 = (bf16[1536,768]{1,0:T(8,128)(2,1)S(1)}, bf16[1536,768]{1,0:T(8,128)(2,1)}, u32[]{:S(2)}, u32[]{:S(2)}) collective-permute-start(bf16[1536,768]{1,0:T(8,128)(2,1)S(1)} %collective-permute-done.own), channel_id=1, source_target_pairs={{8,24},{10,26},{12,28},{14,30},{17,1},{19,3},{21,5},{23,7},{24,40}... | collective-permute-start | bytes 7077896 | tf_op jit(solution)/shard_map/ppermute | solution.py:254
  52.4 55.5 %collective-permute-start.7 = (bf16[1536,768]{1,0:T(8,128)(2,1)}, bf16[1536,768]{1,0:T(8,128)(2,1)}, u32[]{:S(2)}, u32[]{:S(2)}) collective-permute-start(bf16[1536,768]{1,0:T(8,128)(2,1)} %collective-permute-done.3.refs_0_), channel_id=1, source_target_pairs={{0,1},{2,3},{4,5},{6,7},{9,8},{11,10},{13,12},{15,14},{16,17},{18,... | collective-permute-start | bytes 7077896 | tf_op jit(solution)/shard_map/ppermute | solution.py:254
  98.6 11.7 %copy-start.6 = (bf16[1552,384]{1,0:T(8,128)(2,1)}, bf16[1552,384]{1,0:T(8,128)(2,1)S(1)}, u32[]{:S(2)}) copy-start(bf16[1552,384]{1,0:T(8,128)(2,1)S(1)} %collective-permute-done.2.query) | copy-start | bytes 3575812
  98.6 11.7 %collective-permute-start.5 = (bf16[1536,768]{1,0:T(8,128)(2,1)}, bf16[1536,768]{1,0:T(8,128)(2,1)}, u32[]{:S(2)}, u32[]{:S(2)}) collective-permute-start(bf16[1536,768]{1,0:T(8,128)(2,1)} %collective-permute-done.4.refs_3_), channel_id=1, source_target_pairs={{1,0},{3,2},{5,4},{7,6},{8,9},{10,11},{12,13},{14,15},{17,16},{19,... | collective-permute-start | bytes 7077896 | tf_op jit(solution)/shard_map/ppermute | solution.py:254
  133.8 20.0 %collective-permute-start.10 = (bf16[1536,256]{1,0:T(8,128)(2,1)}, bf16[1536,256]{1,0:T(8,128)(2,1)}, u32[]{:S(2)}, u32[]{:S(2)}) collective-permute-start(bf16[1536,256]{1,0:T(8,128)(2,1)} %attend.2), channel_id=1, source_target_pairs={{0,0},{1,8},{2,2},{3,10},{4,4},{5,12},{6,6},{7,14},{8,1},{9,9},{10... | collective-permute-start | bytes 2359304 | tf_op jit(solution)/shard_map/ppermute | solution.py:254
  153.8 18.1 %all-to-all-start.1 = ((bf16[8,192,256]{2,1,0:T(8,128)(2,1)}), bf16[8,192,256]{2,1,0:T(8,128)(2,1)S(1)}, u32[]{:S(2)}, u32[]{:S(2)}) async-start(bf16[8,192,256]{2,1,0:T(8,128)(2,1)} %bitcast.3), calls=%async_computation.1 | async-start | bytes 1572864 | tf_op jit(solution)/shard_map/all_to_all | solution.py:290
  159.5 12.2 %collective-permute-start.9 = (bf16[1536,128]{1,0:T(8,128)(2,1)}, bf16[1536,128]{1,0:T(8,128)(2,1)}, u32[]{:S(2)}, u32[]{:S(2)}) collective-permute-start(bf16[1536,128]{1,0:T(8,128)(2,1)} %attend.3), channel_id=1, source_target_pairs={{0,0},{1,8},{2,2},{3,10},{4,4},{5,12},{6,6},{7,14},{8,1},{9,9},{10... | collective-permute-start | bytes 1179656 | tf_op jit(solution)/shard_map/ppermute | solution.py:254
  171.8 4.7 %copy-start = (bf16[8,192,256]{2,1,0:T(8,128)(2,1)}, bf16[8,192,256]{2,1,0:T(8,128)(2,1)S(1)}, u32[]{:S(2)}) copy-start(bf16[8,192,256]{2,1,0:T(8,128)(2,1)S(1)} %all-to-all-done.1.rows) | copy-start | bytes 2359300
  171.8 12.8 %all-to-all-start = ((bf16[8,192,128]{2,1,0:T(8,128)(2,1)}), bf16[8,192,128]{2,1,0:T(8,128)(2,1)S(1)}, u32[]{:S(2)}, u32[]{:S(2)}) async-start(bf16[8,192,128]{2,1,0:T(8,128)(2,1)} %bitcast.1), calls=%async_computation | async-start | bytes 786432 | tf_op jit(solution)/shard_map/all_to_all | solution.py:290
  184.6 0.8 copy-start.1
Sparse Core Ops, SparseCore 0:
  9.2 101.8 all-gather.1
